TPU v7x, 32 devices: a whole 2x2x4 slice. The times are simulated.
32 devices in a mesh: row: 4 (over z), col: 4 (over x, core), depth: 2 (over y).
Axes of the slice: x: 2, y: 2, z: 4, core: 2. Of those that a mesh axis runs over, the one named last changes fastest.
Arguments:
- block_values: bfloat16 [8, 4, 16, 128, 128], P(('row', 'depth'), 'col'), may hold values from 0.0049743652 to 0.5
- block_cols: int32 [8, 4, 16], P(('row', 'depth'), 'col'), may hold values from 0 to 31, as said below
- live_count: int32 [8, 4], P(('row', 'depth'), 'col'), may hold values from 8 to 16, as said below
- out_pattern: int32 [4, 4, 8, 2], P('row', 'col'), may hold values from 0 to 31, as said below
Outputs:
- squared_log: bfloat16 [4, 4, 8, 128, 128], P('row', 'col', 'depth')
Inputs may be any that keep to these rules, and one draw needn't show every extreme that they name: Block row i's blocks are its first live_count slots; in every draw some block row is full. `block_cols`: the slots of one block row name distinct block columns. Call (k // 4) % 2 the depth part of a block index k and k // 8 its column group. Among the live slots of one block row at most 8 name a column in any one depth part and at most 4 in any one column group; both bounds are reached in every draw. The 8 entries of out_pattern[r, c] are distinct pairs (i, j) with i // 8 == r and j // 8 == c.
All inputs are finite; a program needn't handle non-finite values.
Results may differ from a plain program's by a relative error of at most 0.001.
Values may be sent and summed in bfloat16 or wider, within the bound.
A program may use at most 128 MiB of HBM per device.

v0:
```python
import math

import jax
import jax.numpy as jnp
from jax import lax
from jax.sharding import PartitionSpec as P


def pack_slots(values, col_ids, targets, is_live, part_count, capacity):
    row_count = col_ids.shape[0]
    block_size = values.shape[-1]
    chosen = (
        targets[:, :, None] == jnp.arange(part_count, dtype=jnp.int32)[None, None, :]
    ) & is_live[:, :, None]
    running = jnp.cumsum(chosen.astype(jnp.int32), axis=1) - 1
    order_in = jnp.sum(jnp.where(chosen, running, 0), axis=2)
    row_ids = jnp.arange(row_count, dtype=jnp.int32)[:, None]
    total = part_count * row_count * capacity
    position = (targets * row_count + row_ids) * capacity + order_in
    position = jnp.where(is_live, position, total).reshape(-1)
    packed = jnp.zeros((total, block_size, block_size), values.dtype)
    packed = packed.at[position].set(values.reshape(-1, block_size, block_size), mode="drop")
    packed_cols = (
        jnp.full((total,), -1, jnp.int32).at[position].set(col_ids.reshape(-1), mode="drop")
    )
    return (
        packed.reshape(part_count, row_count, capacity, block_size, block_size),
        packed_cols.reshape(part_count, row_count, capacity),
    )


def body(block_values, block_cols, live_count, out_pattern):
    depths = lax.axis_size("depth")
    columns = lax.axis_size("col")
    row_groups = lax.axis_size("row")
    row_index = lax.axis_index("row")
    rows_dev = block_values.shape[1]
    slot_count = block_values.shape[2]
    block_size = block_values.shape[3]
    group_rows = columns * rows_dev
    group_count = row_groups * depths
    total_rows = group_count * group_rows
    col_block = total_rows // columns
    pair_size = group_count // columns
    cap_left = slot_count // depths
    cap_right = pair_size * (slot_count // group_count) + min(pair_size, slot_count % group_count)
    values = block_values.reshape(rows_dev, slot_count, block_size, block_size)
    col_ids = block_cols.reshape(rows_dev, slot_count)
    counts = live_count.reshape(rows_dev)
    is_live = jnp.arange(slot_count, dtype=jnp.int32)[None, :] < counts[:, None]
    left_vals, left_cols = pack_slots(
        values, col_ids, col_ids // group_rows % depths, is_live, depths, cap_left
    )
    left_vals, left_cols = (
        lax.all_to_all(left_vals, "depth", split_axis=0, concat_axis=0, tiled=True),
        lax.all_to_all(left_cols, "depth", split_axis=0, concat_axis=0, tiled=True),
    )
    left_vals, left_cols = (
        lax.all_gather(left_vals[None], "col", axis=0, tiled=True),
        lax.all_gather(left_cols[None], "col", axis=0, tiled=True),
    )
    left_shape = left_cols.shape
    source_col = lax.broadcasted_iota(jnp.int32, left_shape, 0)
    source_depth = lax.broadcasted_iota(jnp.int32, left_shape, 1)
    source_row = lax.broadcasted_iota(jnp.int32, left_shape, 2)
    left_rows = (
        (row_index * depths + source_depth) * group_rows + source_col * rows_dev + source_row
    ).reshape(-1)
    left_flat = left_vals.reshape(-1, block_size, block_size)
    left_ids = left_cols.reshape(-1)
    right_vals, right_cols = pack_slots(
        values, col_ids, col_ids // col_block, is_live, columns, cap_right
    )
    right_vals, right_cols = (
        lax.all_to_all(right_vals, "col", split_axis=0, concat_axis=0, tiled=True),
        lax.all_to_all(right_cols, "col", split_axis=0, concat_axis=0, tiled=True),
    )
    right_vals, right_cols = (
        lax.all_gather(right_vals[None], "row", axis=0, tiled=True),
        lax.all_gather(right_cols[None], "row", axis=0, tiled=True),
    )
    right_flat = right_vals.reshape(-1, cap_right, block_size, block_size)
    right_ids = right_cols.reshape(-1, cap_right)
    safe_inner = jnp.maximum(left_ids, 0)
    inner_block = safe_inner // group_rows
    inner_within = safe_inner % group_rows
    right_index = (
        inner_block // depths * columns + inner_within // rows_dev
    ) * rows_dev + inner_within % rows_dev
    pattern_rows = out_pattern[0, 0, :, 0]
    pattern_cols = out_pattern[0, 0, :, 1]
    pattern_len = pattern_rows.shape[0]
    pattern_ids = jnp.arange(pattern_len, dtype=jnp.int32)
    slot_total = left_ids.shape[0]
    step_len = math.gcd(slot_total, 32)
    turns = slot_total // step_len

    def one_turn(partial_value, turn):
        begin = turn * step_len
        left_part = lax.dynamic_slice_in_dim(left_flat, begin, step_len, 0)
        left_part_ids = lax.dynamic_slice_in_dim(left_ids, begin, step_len, 0)
        left_part_rows = lax.dynamic_slice_in_dim(left_rows, begin, step_len, 0)
        picked_index = lax.dynamic_slice_in_dim(right_index, begin, step_len, 0)
        right_part = jnp.take(right_flat, picked_index, axis=0)
        right_part_ids = jnp.take(right_ids, picked_index, axis=0)
        usable = (left_part_ids >= 0)[:, None] & (right_part_ids >= 0)
        matched = (
            (left_part_rows[:, None, None] == pattern_rows[None, None, :])
            & (right_part_ids[:, :, None] == pattern_cols[None, None, :])
            & usable[:, :, None]
        )
        target = jnp.where(
            jnp.any(matched, axis=2),
            jnp.sum(jnp.where(matched, pattern_ids[None, None, :], 0), axis=2),
            pattern_len,
        )
        products = jnp.einsum(
            "lab,lsbc->lsac", left_part, right_part, preferred_element_type=jnp.float32
        )
        summed = jax.ops.segment_sum(
            products.reshape(-1, block_size, block_size),
            target.reshape(-1),
            num_segments=pattern_len + 1,
        )
        return (partial_value + summed[:pattern_len], None)

    partial_sum = jnp.zeros((pattern_len, block_size, block_size), jnp.float32)
    partial_sum, _ = lax.scan(one_turn, partial_sum, jnp.arange(turns, dtype=jnp.int32))
    share = lax.psum_scatter(partial_sum[None, None], "depth", scatter_dimension=2, tiled=True)
    return jnp.log1p(share).astype(jnp.bfloat16)


def solution(mesh):
    in_specs = (
        P(("row", "depth"), "col", None, None, None),
        P(("row", "depth"), "col", None),
        P(("row", "depth"), "col"),
        P("row", "col", None, None),
    )
    out_specs = P("row", "col", "depth", None, None)
    return jax.shard_map(body, mesh=mesh, in_specs=in_specs, out_specs=out_specs, check_vma=False)
```

profile of v0, /device:TPU:0, one launch (start us, length us, event | category | flops | bytes accessed | tf_op | source)
XLA Modules:
  0.0 200.5 jit_solution(16666299593631244725)
XLA Ops:
  9.3 2.1 %scatter_fusion.2 = bf16[16,128,128]{2,1,0:T(8,128)(2,1)S(1)} fusion(bf16[16,128,128]{2,1,0:T(8,128)(2,1)S(1)} %broadcast.692.clone.1, s32[16]{0:T(128)S(1)} %get-tuple-element.191, bf16[16,128,128]{2,1,0:T(8,128)(2,1)} %bitcast.76), kind=kCustom, calls=%fused_computation.6 | custom fusion | bytes 1572928 | tf_op jit(solution)/shard_map/scatter | solution.py:22
  11.4 12.6 %all_to_all.20 = bf16[2,1,8,128,128]{4,3,2,1,0:T(8,128)(2,1)} all-to-all(bf16[2,1,8,128,128]{4,3,2,1,0:T(8,128)(2,1)S(1)} %bitcast.75), channel_id=1, replica_groups=mesh['row'=4,'col'=4,'depth'=2] {'depth'}, dimensions={0} | all-to-all | bytes 1048576 | tf_op jit(solution)/shard_map/all_to_all | solution.py:55
  24.2 1.1 scatter_fusion.1
  25.4 14.9 %all_to_all.21 = bf16[4,1,4,128,128]{4,3,2,1,0:T(8,128)(2,1)} all-to-all(bf16[4,1,4,128,128]{4,3,2,1,0:T(8,128)(2,1)S(1)} %bitcast.74), channel_id=1, replica_groups=mesh['row'=4,'col'=4,'depth'=2] {'col'}, dimensions={0} | all-to-all | bytes 1048576 | tf_op jit(solution)/shard_map/all_to_all | solution.py:75
  40.3 0.8 scatter_custom_fusion.1
  41.8 3.2 %all-to-all-start = ((s32[2,1,8]{2,1,0:T(1,128)}), s32[2,1,8]{2,1,0:T(1,128)S(1)}, u32[]{:S(2)}, u32[]{:S(2)}) async-start(s32[2,1,8]{2,1,0:T(1,128)} %bitcast.5), calls=%async_computation | async-start | bytes 2048 | tf_op jit(solution)/shard_map/all_to_all | solution.py:56
  45.0 0.8 scatter_custom_fusion.2
  46.6 2.0 all-to-all-done
  48.6 3.2 %all-to-all-start.1 = ((s32[4,1,4]{2,1,0:T(1,128)}), s32[4,1,4]{2,1,0:T(1,128)S(1)}, u32[]{:S(2)}, u32[]{:S(2)}) async-start(s32[4,1,4]{2,1,0:T(1,128)} %bitcast.8), calls=%async_computation.1 | async-start | bytes 4096 | tf_op jit(solution)/shard_map/all_to_all | solution.py:76
  51.8 5.1 %all-gather = s32[8,1,8]{2,1,0:T(1,128)S(1)} all-gather(s32[2,1,8]{2,1,0:T(1,128)S(1)} %all-to-all-done), channel_id=2, replica_groups=mesh['row'=4,'col'=4,'depth'=2] {'col'}, dimensions={0}, use_global_device_ids=true | all-gather | bytes 320 | tf_op jit(solution)/shard_map/all_gather | solution.py:60
  58.3 13.4 %all-gather.1 = s32[16,1,4]{2,1,0:T(1,128)S(1)} all-gather(s32[4,1,4]{2,1,0:T(1,128)S(1)} %all-to-all-done.1), channel_id=3, replica_groups=mesh['row'=4,'col'=4,'depth'=2] {'row'}, dimensions={0}, use_global_device_ids=true | all-gather | bytes 320 | tf_op jit(solution)/shard_map/all_gather | solution.py:80
  71.7 25.5 %all-gather.7.cloned.1.call-done = bf16[16,1,4,128,128]{4,3,2,1,0:T(8,128)(2,1)} async-done(((bf16[4,1,4,128,128]{4,3,2,1,0:T(8,128)(2,1)}), bf16[16,1,4,128,128]{4,3,2,1,0:T(8,128)(2,1)}) %all-gather.7.cloned.1.call-update) | async-done | bytes 2097168 | tf_op jit(solution)/shard_map/all_gather | solution.py:79
  97.2 80.8 %while.11 = (s32[]{:T(128)}, f32[8,128,128]{2,1,0:T(8,128)S(1)}, s32[2]{0:T(128)S(1)}, s32[64]{0:T(128)S(1)}, s32[1,1,8,1]{2,3,1,0:T(1,128)S(1)}, /*index=5*/s32...) while((s32[]{:T(128)}, f32[8,128,128]{2,1,0:T(8,128)S(1)}, ...), condition=%wide.region_12.13_spmd.clone, body=%wide.region_8.12_spmd.clone.sunk | while | flops 541338368 | bytes 74530272 | solution.py:128
  98.6 4.8 %gather_fusion.1 = bf16[32,4,128,128]{3,2,1,0:T(8,128)(2,1)} fusion(bf16[16,4,128,128]{3,2,1,0:T(8,128)(2,1)} %get-tuple-element.312, s32[1024]{0:T(1024)S(1)} %pad_clamp_fusion.2), kind=kCustom, calls=%fused_computation.1.clone.clone.1 | custom fusion | bytes 8388736 | tf_op jit(solution)/shard_map/while/body/eval_jaxpr/jit(_take)/gather | solution.py:104
  103.4 6.8 %fusion.37 = f32[32,4,128,128]{3,2,1,0:T(8,128)} fusion(bf16[32,4,128,128]{3,2,1,0:T(8,128)(2,1)} %gather_fusion.1, pred[32]{0:T(512)(128)(4,1)S(1)} %get-tuple-element.268, bf16[64,128,128]{2,1,0:T(8,128)(2,1)S(1)} %copy-done.1, s32[]{:T(128)S(6)} %select_n.292), kind=kOutput, calls=%fused_computation.8.clone.1 | convolution fusion | flops 538968064 | bytes 13632004 | tf_op jit(solution)/shard_map/while/body/eval_jaxpr/lab,lsbc->lsac/dot_general | solution.py:117
  110.2 9.0 %copy.44 = f32[128,128,128]{2,1,0:T(8,128)} copy(f32[128,128,128]{1,2,0:T(8,128)} %bitcast.69) | data formatting | bytes 16777216 | tf_op jit(solution)/shard_map/while/body/eval_jaxpr/reshape | solution.py:121
  120.5 17.0 %scatter_fusion = f32[9,128,128]{2,1,0:T(8,128)S(1)} fusion(f32[9,128,128]{2,1,0:T(8,128)S(1)} %broadcast.738, s32[128]{0:T(128)S(1)} %reshape.896, f32[128,128,128]{2,1,0:T(8,128)} %copy.44), kind=kCustom, calls=%fused_computation.2.clone.clone.1 | custom fusion | flops 2097152 | bytes 25166336 | tf_op jit(solution)/shard_map/while/body/eval_jaxpr/scatter-add | solution.py:120
  139.0 4.8 %gather_fusion.1 = bf16[32,4,128,128]{3,2,1,0:T(8,128)(2,1)} fusion(bf16[16,4,128,128]{3,2,1,0:T(8,128)(2,1)} %get-tuple-element.312, s32[1024]{0:T(1024)S(1)} %pad_clamp_fusion.2), kind=kCustom, calls=%fused_computation.1.clone.clone.1 | custom fusion | bytes 8388736 | tf_op jit(solution)/shard_map/while/body/eval_jaxpr/jit(_take)/gather | solution.py:104
  143.8 6.8 %fusion.37 = f32[32,4,128,128]{3,2,1,0:T(8,128)} fusion(bf16[32,4,128,128]{3,2,1,0:T(8,128)(2,1)} %gather_fusion.1, pred[32]{0:T(512)(128)(4,1)S(1)} %get-tuple-element.268, bf16[64,128,128]{2,1,0:T(8,128)(2,1)S(1)} %copy-done.1, s32[]{:T(128)S(6)} %select_n.292), kind=kOutput, calls=%fused_computation.8.clone.1 | convolution fusion | flops 538968064 | bytes 13632004 | tf_op jit(solution)/shard_map/while/body/eval_jaxpr/lab,lsbc->lsac/dot_general | solution.py:117
  150.6 9.0 %copy.44 = f32[128,128,128]{2,1,0:T(8,128)} copy(f32[128,128,128]{1,2,0:T(8,128)} %bitcast.69) | data formatting | bytes 16777216 | tf_op jit(solution)/shard_map/while/body/eval_jaxpr/reshape | solution.py:121
  160.9 17.0 %scatter_fusion = f32[9,128,128]{2,1,0:T(8,128)S(1)} fusion(f32[9,128,128]{2,1,0:T(8,128)S(1)} %broadcast.738, s32[128]{0:T(128)S(1)} %reshape.896, f32[128,128,128]{2,1,0:T(8,128)} %copy.44), kind=kCustom, calls=%fused_computation.2.clone.clone.1 | custom fusion | flops 2097152 | bytes 25166336 | tf_op jit(solution)/shard_map/while/body/eval_jaxpr/scatter-add | solution.py:120
  178.1 0.8 copy-done
  178.9 13.4 %reduce-scatter.2.cloned.1.call-done = f32[1,1,4,128,128]{4,3,2,1,0:T(8,128)} async-done(((f32[1,1,8,128,128]{4,3,2,1,0:T(8,128)}), f32[1,1,4,128,128]{4,3,2,1,0:T(8,128)}) %reduce-scatter.2.cloned.1.call-update) | async-done | bytes 262160 | tf_op jit(solution)/shard_map/reduce_scatter | solution.py:129
  192.3 1.7 log-plus-one_convert_fusion
  (70 shorter events, 9.4 us)
Async XLA Ops:
  6.5 17.7 %copy-start.2 = (bf16[1,1,16,128,128]{4,3,2,1,0:T(8,128)(2,1)S(1)}, bf16[1,1,16,128,128]{4,3,2,1,0:T(8,128)(2,1)}, u32[]{:S(2)}) copy-start(bf16[1,1,16,128,128]{4,3,2,1,0:T(8,128)(2,1)} %param.6) | copy-start | bytes 1572868
  6.5 40.0 %copy-start.3 = (s32[1,1,8,2]{2,3,1,0:T(2,128)S(1)}, s32[1,1,8,2]{2,3,1,0:T(2,128)}, u32[]{:S(2)}) copy-start(s32[1,1,8,2]{2,3,1,0:T(2,128)} %param.9) | copy-start | bytes 196
  6.5 65.2 %all-gather.9.cloned.1.call-start = ((), (), s32[]{:S(2)}) async-start(), calls=%async_computation.7 | async-start | bytes 2621440 | tf_op jit(solution)/shard_map/all_gather | solution.py:59
  24.0 73.2 %all-gather.7.cloned.1.call-start = ((), (), s32[]{:S(2)}) async-start(), calls=%async_computation.6 | async-start | bytes 2621440 | tf_op jit(solution)/shard_map/all_gather | solution.py:79
  41.8 6.8 %all-to-all-start = ((s32[2,1,8]{2,1,0:T(1,128)}), s32[2,1,8]{2,1,0:T(1,128)S(1)}, u32[]{:S(2)}, u32[]{:S(2)}) async-start(s32[2,1,8]{2,1,0:T(1,128)} %bitcast.5), calls=%async_computation | async-start | bytes 2048 | tf_op jit(solution)/shard_map/all_to_all | solution.py:56
  48.6 9.8 %all-to-all-start.1 = ((s32[4,1,4]{2,1,0:T(1,128)}), s32[4,1,4]{2,1,0:T(1,128)S(1)}, u32[]{:S(2)}, u32[]{:S(2)}) async-start(s32[4,1,4]{2,1,0:T(1,128)} %bitcast.8), calls=%async_computation.1 | async-start | bytes 4096 | tf_op jit(solution)/shard_map/all_to_all | solution.py:76
  51.8 140.5 %reduce-scatter.2.cloned.1.call-start = ((), (), s32[]{:S(2)}) async-start(), calls=%async_computation.5 | async-start | bytes 786432 | tf_op jit(solution)/shard_map/reduce_scatter | solution.py:129
  98.6 4.8 %copy-start.1 = (bf16[64,128,128]{2,1,0:T(8,128)(2,1)S(1)}, bf16[64,128,128]{2,1,0:T(8,128)(2,1)}, u32[]{:S(2)}) copy-start(bf16[64,128,128]{2,1,0:T(8,128)(2,1)} %get-tuple-element.313) | copy-start | bytes 6291460 | tf_op jit(solution)/shard_map/while
  139.0 4.8 %copy-start.1 = (bf16[64,128,128]{2,1,0:T(8,128)(2,1)S(1)}, bf16[64,128,128]{2,1,0:T(8,128)(2,1)}, u32[]{:S(2)}) copy-start(bf16[64,128,128]{2,1,0:T(8,128)(2,1)} %get-tuple-element.313) | copy-start | bytes 6291460 | tf_op jit(solution)/shard_map/while
  178.1 0.8 copy-start
Sparse Core Ops, SparseCore 0:
  24.2 25.7 all-gather.8
  51.5 45.6 all-gather.6
  179.0 13.2 reduce-scatter.1
where the time goes:
time: 202 us; the launch traced here: 200 us
  blocking collectives  46 us (23%)
  waiting for transfers between devices  40.9 us (20%)
  other arithmetic  39.5 us (20%)
  local copies, waits for them, and re-layouts  38.5 us (19%)
  between operations  14 us (7%)
  matrix products  13.6 us (7%)
  starting transfers between devices  6.52 us (3%)
    scatter-add x2, other arithmetic, one_turn(): jax.ops.segment_sum(products.reshape(-1, block_size, block_size), target....  34 us
    all_gather x1, waiting for transfers between devices, body(): lax.all_gather(right_vals[None], 'row', axis=0, tiled=True)  25.5 us
    reshape x2, local copies, waits for them, and re-layouts, one_turn(): products.reshape(-1, block_size, block_size)  18 us
    all_to_all x1, blocking collectives, body(): lax.all_to_all(right_vals, 'col', split_axis=0, concat_axis=0, tiled=True)  14.9 us
    dot_general x2, matrix products, one_turn(): jnp.einsum('lab,lsbc->lsac', left_part, right_part, preferred_element_typ...  13.6 us
    all_gather x1, blocking collectives, body(): lax.all_gather(right_cols[None], 'row', axis=0, tiled=True)  13.4 us
    reduce_scatter x1, waiting for transfers between devices, body(): lax.psum_scatter(partial_sum[None, None], 'depth', scatter_dimension=2, t...  13.4 us
    all_to_all x1, blocking collectives, body(): lax.all_to_all(left_vals, 'depth', split_axis=0, concat_axis=0, tiled=True)  12.6 us
  transfers between devices with their start and end apart: 5, of which 3 were waited for; matrix products, arithmetic and copies ran while one was open for 3% of the time, Pallas kernels for 0%

commit v1 on v0

v1 whole, which is shorter than its diff:
```python
import functools

import jax
import jax.numpy as jnp
from jax import lax
from jax.experimental import pallas as pl
from jax.experimental.pallas import tpu as pltpu
from jax.sharding import PartitionSpec as P

MESH = pl.DeviceIdType.MESH


def kernel(
    dims,
    index_ref,
    pattern_ref,
    meta_ref,
    values_ref,
    out_ref,
    left_stage,
    right_stage,
    left_buf,
    right_buf,
    left_meta,
    right_meta,
    left_ids,
    right_ids,
    partial,
    arrived,
    send_sem,
    left_sem,
    right_sem,
    meta_sems,
    local_sems,
    part_send,
    part_recv,
):
    rows, cols, depths, cap_left, cap_right = dims
    r, c, d = lax.axis_index("row"), lax.axis_index("col"), lax.axis_index("depth")
    left_me = d * cols + c
    right_me = r * cols + c
    share = out_ref.shape[0]
    left_total = depths * cap_left
    lefts = cols * depths
    rights = rows * cols
    zero_slot = rights * cap_right

    barrier = pltpu.get_barrier_semaphore()
    left_peers = [(m, e) for m in range(cols) for e in range(depths) if m or e]
    right_peers = [(m, n) for n in range(rows) for m in range(cols) if m or n]

    def left_peer(m, e):
        return (r, lax.rem(c + m, cols), lax.rem(d + e, depths))

    def right_peer(m, n):
        return (lax.rem(r + n, rows), lax.rem(c + m, cols), d)

    greeted = [left_peer(m, e) for m, e in left_peers]
    greeted += [right_peer(m, n) for m, n in right_peers if n]
    for peer in greeted:
        pl.semaphore_signal(barrier, inc=1, device_id=peer, device_id_type=MESH)

    for m in range(cols):
        cc = lax.rem(c + m, cols)
        for q in range(cap_right):
            block = values_ref[index_ref[0, left_total + cc * cap_right + q]]
            right_stage[m, q] = block
            if m == 0:
                right_buf[right_me * cap_right + q] = block
    for e in range(depths):
        dd = lax.rem(d + e, depths)
        for q in range(cap_left):
            block = values_ref[index_ref[0, dd * cap_left + q]]
            left_stage[e, q] = block
            if e == 0:
                left_buf[left_me * cap_left + q] = block
    left_meta[left_me] = meta_ref[0]
    right_meta[right_me] = meta_ref[0]
    right_buf[zero_slot] = jnp.zeros(right_buf.shape[1:], right_buf.dtype)

    pl.semaphore_wait(barrier, len(greeted))

    for n in range(rows - 1, -1, -1):
        for m in range(cols):
            if m or n:
                pltpu.make_async_remote_copy(
                    src_ref=right_stage.at[m],
                    dst_ref=right_buf.at[pl.ds(right_me * cap_right, cap_right)],
                    send_sem=send_sem.at[0],
                    recv_sem=right_sem,
                    device_id=right_peer(m, n),
                    device_id_type=MESH,
                ).start()
    for m, e in left_peers:
        pltpu.make_async_remote_copy(
            src_ref=left_stage.at[e],
            dst_ref=left_buf.at[pl.ds(left_me * cap_left, cap_left)],
            send_sem=send_sem.at[1],
            recv_sem=left_sem,
            device_id=left_peer(m, e),
            device_id_type=MESH,
        ).start()
    for m, e in left_peers:
        pltpu.make_async_remote_copy(
            src_ref=meta_ref,
            dst_ref=left_meta.at[pl.ds(left_me, 1)],
            send_sem=send_sem.at[2],
            recv_sem=meta_sems.at[0],
            device_id=left_peer(m, e),
            device_id_type=MESH,
        ).start()
    for m, n in right_peers:
        pltpu.make_async_remote_copy(
            src_ref=meta_ref,
            dst_ref=right_meta.at[pl.ds(right_me, 1)],
            send_sem=send_sem.at[3],
            recv_sem=meta_sems.at[1],
            device_id=right_peer(m, n),
            device_id_type=MESH,
        ).start()

    def wait_all(ref, sem):
        pltpu.make_async_copy(ref, ref, sem).wait()

    wait_all(left_meta.at[pl.ds(0, lefts - 1)], meta_sems.at[0])
    wait_all(right_meta.at[pl.ds(0, rights - 1)], meta_sems.at[1])
    left_copy = pltpu.make_async_copy(left_meta, left_ids, local_sems.at[0])
    right_copy = pltpu.make_async_copy(right_meta, right_ids, local_sems.at[1])
    left_copy.start()
    right_copy.start()
    left_copy.wait()
    right_copy.wait()
    wait_all(left_buf.at[pl.ds(0, (lefts - 1) * cap_left)], left_sem)
    wait_all(right_buf.at[pl.ds(0, (rights - 1) * cap_right)], right_sem)

    def one_entry(p):
        i = lax.rem(pattern_ref[0, 0, p, 0], lefts)
        j = pattern_ref[0, 0, p, 1]
        left_parts, right_parts = [], []
        for q in range(cap_left):
            inner = left_ids[i, 0, d * cap_left + q]
            place = jnp.maximum(inner, 0)
            at = jnp.int32(zero_slot)
            for t in range(cap_right):
                found = right_ids[place, 0, left_total + c * cap_right + t]
                at = jnp.where((inner >= 0) & (found == j), place * cap_right + t, at)
            left_parts.append(left_buf[i * cap_left + q])
            right_parts.append(right_buf[at])
        return jnp.dot(
            jnp.concatenate(left_parts, axis=1),
            jnp.concatenate(right_parts, axis=0),
            preferred_element_type=jnp.float32,
        )

    copies = []
    for e in range(1, depths + 1):
        dd = lax.rem(d + e, depths)

        def step(u, carry, e=e, dd=dd):
            partial[e - 1, u] = one_entry(dd * share + u)
            return carry

        lax.fori_loop(0, share, step, 0)
        if e < depths:
            copy = pltpu.make_async_remote_copy(
                src_ref=partial.at[e - 1],
                dst_ref=arrived.at[e - 1],
                send_sem=part_send.at[e - 1],
                recv_sem=part_recv.at[e - 1],
                device_id=(r, c, dd),
                device_id_type=MESH,
            )
            copy.start()
            copies.append(copy)
    total = partial[depths - 1]
    for e, copy in enumerate(copies):
        copy.wait_recv()
        total = total + arrived[e]
    out_ref[...] = total
    for copy in copies:
        copy.wait_send()
    sent = rights - 1
    wait_all(right_buf.at[pl.ds(0, sent * cap_right)], send_sem.at[0])
    sent = lefts - 1
    wait_all(left_buf.at[pl.ds(0, sent * cap_left)], send_sem.at[1])
    wait_all(left_meta.at[pl.ds(0, lefts - 1)], send_sem.at[2])
    wait_all(right_meta.at[pl.ds(0, rights - 1)], send_sem.at[3])


def body(block_values, block_cols, live_count, out_pattern):
    depths = lax.axis_size("depth")
    cols = lax.axis_size("col")
    rows = lax.axis_size("row")
    slots, size = block_values.shape[2], block_values.shape[3]
    groups = rows * depths
    col_block = groups
    pair = groups // cols
    cap_left = slots // depths
    cap_right = pair * (slots // groups) + min(pair, slots % groups)
    share = out_pattern.shape[2] // depths

    ids = block_cols.reshape(slots)
    order = jnp.arange(slots, dtype=jnp.int32)
    live = order < live_count.reshape(1)

    def table(part, parts, cap, payload):
        same = (part[:, None] == part[None, :]) & live[None, :]
        rank = jnp.sum((same & (order[None, :] < order[:, None])).astype(jnp.int32), axis=1)
        place = jnp.where(live, part * cap + rank, -1)
        hit = place[:, None] == jnp.arange(parts * cap, dtype=jnp.int32)[None, :]
        index = jnp.sum(jnp.where(hit, order[:, None], 0), axis=0)
        held = jnp.sum(jnp.where(hit, payload[:, None] + 1, 0), axis=0) - 1
        return index, held

    inner_place = ids // (cols * depths) * cols + ids % cols
    left_index, left_held = table(ids // cols % depths, depths, cap_left, inner_place)
    right_index, right_held = table(ids // col_block, cols, cap_right, ids)
    index = jnp.concatenate([left_index, right_index])[None]
    held = jnp.concatenate([left_held, right_held])
    meta = jnp.pad(held, (0, 128 - held.shape[0])).reshape(1, 1, 128)

    lefts, rights = cols * depths, rows * cols
    block = (size, size)
    bf16, i32 = jnp.bfloat16, jnp.int32
    vmem, smem = pltpu.VMEM, pltpu.SMEM
    dma = pltpu.SemaphoreType.DMA
    total = pl.pallas_call(
        functools.partial(kernel, (rows, cols, depths, cap_left, cap_right)),
        out_shape=jax.ShapeDtypeStruct((share,) + block, jnp.float32),
        in_specs=[pl.BlockSpec(memory_space=smem)] * 2 + [pl.BlockSpec(memory_space=vmem)] * 2,
        out_specs=pl.BlockSpec(memory_space=vmem),
        scratch_shapes=[
            vmem((depths, cap_left) + block, bf16),
            vmem((cols, cap_right) + block, bf16),
            vmem((lefts * cap_left,) + block, bf16),
            vmem((rights * cap_right + 1,) + block, bf16),
            vmem((lefts, 1, 128), i32),
            vmem((rights, 1, 128), i32),
            smem((lefts, 1, 128), i32),
            smem((rights, 1, 128), i32),
            vmem((depths, share) + block, jnp.float32),
            vmem((depths - 1, share) + block, jnp.float32),
            dma((4,)),
            dma,
            dma,
            dma((2,)),
            dma((2,)),
            dma((depths - 1,)),
            dma((depths - 1,)),
        ],
        compiler_params=pltpu.CompilerParams(
            collective_id=0, has_side_effects=True, vmem_limit_bytes=40 * 1024 * 1024
        ),
    )(index, out_pattern, meta, block_values.reshape((slots,) + block))
    return jnp.log1p(total).astype(jnp.bfloat16).reshape((1, 1, share) + block)


def solution(mesh):
    in_specs = (
        P(("row", "depth"), "col", None, None, None),
        P(("row", "depth"), "col", None),
        P(("row", "depth"), "col"),
        P("row", "col", None, None),
    )
    out_specs = P("row", "col", "depth", None, None)
    return jax.shard_map(body, mesh=mesh, in_specs=in_specs, out_specs=out_specs, check_vma=False)
```

time: 202 us -> 67.9 us (0.34)
  Pallas kernels: 0 us -> 63.4 us
  blocking collectives: 46 us -> 0 us
  waiting for transfers between devices: 40.9 us -> 0 us
  other arithmetic: 39.5 us -> 1.22 us
  local copies, waits for them, and re-layouts: 38.5 us -> 2.44 us
  matrix products: 13.6 us -> 0 us
  between operations: 14 us -> 0.7 us
  starting transfers between devices: 6.52 us -> 0 us
    pallas_call x0 -> x1, Pallas kernels: none -> 63.4 us  [body(): pl.pallas_call(functools.partial(kernel, (rows, cols, depths, cap_left, c...]
    scatter-add x2 -> x0, other arithmetic: 34 us -> none  [one_turn(): jax.ops.segment_sum(products.reshape(-1, block_size, block_size), target....]
    all_to_all x2 -> x0, blocking collectives: 27.6 us -> none  [the longest x1 14.9 us: body(): lax.all_to_all(right_vals, 'col', split_axis=0, concat_axis=0, tiled=True)]
    all_gather x2 -> x0, waiting for transfers between devices: 25.5 us -> none  [the longest x1 25.5 us: body(): lax.all_gather(right_vals[None], 'row', axis=0, tiled=True)]
    reshape x5 -> x1, local copies, waits for them, and re-layouts: 19.4 us -> 0.01 us  [body(): meta = jnp.pad(held, (0, 128 - held.shape[0])).reshape(1, 1, 128)]
    all_gather x2 -> x0, blocking collectives: 18.5 us -> none  [the longest x1 13.4 us: body(): lax.all_gather(right_cols[None], 'row', axis=0, tiled=True)]
    dot_general x2 -> x0, matrix products: 13.6 us -> none  [one_turn(): jnp.einsum('lab,lsbc->lsac', left_part, right_part, preferred_element_typ...]
    reduce_scatter x1 -> x0, waiting for transfers between devices: 13.4 us -> none  [body(): lax.psum_scatter(partial_sum[None, None], 'depth', scatter_dimension=2, t...]
  transfers between devices with their start and end apart: 5 -> 0, of which waited for: 3 -> 0; matrix products, arithmetic and copies ran while one was open for 3% -> 0% of each run, Pallas kernels for 0% -> 0%
where the time goes in v1:
time: 67.9 us; the launch traced here: 67.7 us
  Pallas kernels  63.4 us (93%)
  local copies, waits for them, and re-layouts  2.44 us (4%)
  other arithmetic  1.22 us (2%)
  between operations  0.7 us (1%)
    pallas_call x1, Pallas kernels, body(): pl.pallas_call(functools.partial(kernel, (rows, cols, depths, cap_left, c...  63.4 us
    unnamed x7, local copies, waits for them, and re-layouts  2.43 us

profile of v1, /device:TPU:0, one launch (start us, length us, event | category | flops | bytes accessed | tf_op | source)
XLA Modules:
  0.0 67.7 jit_solution(14327916826447089829)
XLA Ops:
  0.7 0.0 copy-start.2
  0.7 0.6 copy-done.2
  1.3 0.2 convert_reduce_fusion.1
  1.5 0.1 select_reduce_fusion
  1.6 0.1 add_bitcast_fusion.index_ref
  1.7 0.1 pad_add_fusion
  1.8 0.0 copy-start.1
  1.8 0.7 copy-done.1
  2.5 0.1 copy.6.pattern_ref
  2.6 0.0 copy-start
  2.6 1.0 %copy-done = bf16[1,1,16,128,128]{4,3,2,1,0:T(8,128)(2,1)S(1)} copy-done((bf16[1,1,16,128,128]{4,3,2,1,0:T(8,128)(2,1)S(1)}, bf16[1,1,16,128,128]{4,3,2,1,0:T(8,128)(2,1)}, u32[]{:S(2)}) %copy-start) | copy-done | bytes 524312
  3.6 63.4 %shard_map.46 = f32[4,128,128]{2,1,0:T(8,128)S(1)} custom-call(s32[1,32]{1,0:T(1,128)S(1)} %add_bitcast_fusion.index_ref, s32[1,1,8,2]{3,2,1,0:T(8,128)S(1)} %copy.6.pattern_ref, s32[1,1,128]{2,1,0:T(1,128)S(1)} %pad_bitcast_fusion.meta_ref, bf16[16,128,128]{2,1,0:T(8,128)(2,1)S(1)} %bitcast.39), custom_call_target="tpu_custom_call" | custom-call | tf_op jit(solution)/shard_map/pallas_call | solution.py:227
  67.0 0.7 %fusion = bf16[1,1,4,128,128]{4,3,2,1,0:T(8,128)(2,1)} fusion(f32[4,128,128]{2,1,0:T(8,128)S(1)} %shard_map.46), kind=kLoop, calls=%fused_computation.1 | loop fusion | flops 65536 | bytes 393216 | tf_op jit(solution)/shard_map/reshape | solution.py:255
  (7 shorter events, 0.0 us)
Async XLA Ops:
  0.7 0.7 copy-start.2
  1.8 0.7 %copy-start.1 = (s32[1,1,8,2]{2,3,1,0:T(2,128)S(1)}, s32[1,1,8,2]{2,3,1,0:T(2,128)}, u32[]{:S(2)}) copy-start(s32[1,1,8,2]{2,3,1,0:T(2,128)} %param.7) | copy-start | bytes 196
  2.6 1.0 %copy-start = (bf16[1,1,16,128,128]{4,3,2,1,0:T(8,128)(2,1)S(1)}, bf16[1,1,16,128,128]{4,3,2,1,0:T(8,128)(2,1)}, u32[]{:S(2)}) copy-start(bf16[1,1,16,128,128]{4,3,2,1,0:T(8,128)(2,1)} %param.4) | copy-start | bytes 1572868

commit v2 on v1

v2 whole, which is shorter than its diff:
```python
import functools

import jax
import jax.numpy as jnp
from jax import lax
from jax.experimental import pallas as pl
from jax.experimental.pallas import tpu as pltpu
from jax.sharding import PartitionSpec as P

MESH = pl.DeviceIdType.MESH


def kernel(
    dims,
    index_ref,
    pattern_ref,
    meta_ref,
    values_ref,
    out_ref,
    left_stage,
    right_stage,
    left_buf,
    left_meta,
    right_meta,
    left_ids,
    right_ids,
    partial,
    arrived,
    left_send,
    left_sem,
    pass_send,
    right_send,
    right_sem,
    line_send,
    meta_send,
    meta_sems,
    local_sems,
    part_send,
    part_recv,
    *planes,
):
    rows, cols, depths, cap_left, cap_right = dims
    r, c, d = lax.axis_index("row"), lax.axis_index("col"), lax.axis_index("depth")
    left_me = d * cols + c
    right_me = r * cols + c
    share = out_ref.shape[0]
    left_total = depths * cap_left
    lefts = cols * depths
    rights = rows * cols
    zero_slot = cols * cap_right
    other_core = c + 1 - 2 * lax.rem(c, 2)

    def remote(src, dst, send, recv, to):
        copy = pltpu.make_async_remote_copy(
            src_ref=src,
            dst_ref=dst,
            send_sem=send,
            recv_sem=recv,
            device_id=to,
            device_id_type=MESH,
        )
        copy.start()
        return copy

    def wait_all(ref, sem):
        pltpu.make_async_copy(ref, ref, sem).wait()

    def chunk(m, source):
        return planes[m].at[pl.ds(source * cap_right, cap_right)]

    def left_chunk(source):
        return left_buf.at[pl.ds(source * cap_left, cap_left)]

    barrier = pltpu.get_barrier_semaphore()
    left_peers = [(m, e) for m in range(cols) for e in range(depths) if m or e]
    right_peers = [(m, n) for n in range(rows) for m in range(cols) if m or n]

    def left_peer(m, e):
        return (r, lax.rem(c + m, cols), lax.rem(d + e, depths))

    def right_peer(m, n):
        return (lax.rem(r + n, rows), lax.rem(c + m, cols), d)

    greeted = [left_peer(m, e) for m, e in left_peers]
    greeted += [right_peer(m, n) for m, n in right_peers if n]
    for peer in greeted:
        pl.semaphore_signal(barrier, inc=1, device_id=peer, device_id_type=MESH)

    for m in range(cols):
        cc = lax.rem(c + m, cols)
        for q in range(cap_right):
            block = values_ref[index_ref[0, left_total + cc * cap_right + q]]
            if m == 0:
                planes[0][c * cap_right + q] = block
            else:
                right_stage[m - 1, q] = block
    for e in range(depths):
        dd = lax.rem(d + e, depths)
        for q in range(cap_left):
            block = values_ref[index_ref[0, dd * cap_left + q]]
            if e == 0:
                left_buf[left_me * cap_left + q] = block
            else:
                left_stage[e - 1, q] = block
    left_meta[left_me] = meta_ref[0]
    right_meta[right_me] = meta_ref[0]
    for m in range(rows):
        planes[m][zero_slot] = jnp.zeros(planes[m].shape[1:], planes[m].dtype)

    pl.semaphore_wait(barrier, len(greeted))

    for m in range(1, cols):
        remote(
            right_stage.at[m - 1],
            chunk(0, c),
            right_send.at[m - 1],
            right_sem.at[0, c],
            right_peer(m, 0),
        )

    def line(rr, m, source):
        copies = []
        plane = (rr + m) % rows
        for step, ahead in ((1, plane <= rr < rows - 1), (-1, plane >= rr > 0)):
            if ahead:
                there = (m - step) % rows
                copies.append(
                    remote(
                        chunk(m, source),
                        chunk(there, source),
                        line_send.at[(step + 1) // 2, m, source],
                        right_sem.at[there, source],
                        (r + step, c, d),
                    )
                )
        return copies

    def at_row(rr, run):
        pl.when(r == rr)(functools.partial(run, rr))

    for rr in range(rows):
        at_row(rr, lambda rr: line(rr, 0, c) and None)

    for e in range(depths):
        for m in range(0, cols, 2):
            if m or e:
                remote(
                    left_chunk(left_me) if e == 0 else left_stage.at[e - 1],
                    left_chunk(left_me),
                    left_send.at[e, m // 2],
                    left_sem.at[left_me],
                    left_peer(m, e),
                )

    for m, e in left_peers:
        remote(meta_ref, left_meta.at[pl.ds(left_me, 1)], meta_send.at[0], meta_sems.at[0], left_peer(m, e))
    for m, n in right_peers:
        remote(meta_ref, right_meta.at[pl.ds(right_me, 1)], meta_send.at[1], meta_sems.at[1], right_peer(m, n))

    def pass_left(source):
        return remote(
            left_chunk(source),
            left_chunk(source),
            pass_send.at[source],
            left_sem.at[source],
            (r, other_core, d),
        )

    passed = [pass_left(left_me)]

    def one_plane(rr, m, p):
        i = pattern_ref[0, p]
        j = pattern_ref[1, p]
        plane = (rr + m) % rows
        left_parts, right_parts = [], []
        for source in range(cols):
            inner = plane * cols + source
            q = lax.rem(left_ids[i, 0, d * rights + inner], 256)
            t = lax.div(right_ids[inner, 0, j], 256)
            at = jnp.where((q > 0) & (t > 0), source * cap_right + t - 1, zero_slot)
            left_parts.append(left_buf[i * cap_left + jnp.maximum(q - 1, 0)])
            right_parts.append(planes[m][at])
        return jnp.dot(
            jnp.concatenate(left_parts, axis=1),
            jnp.concatenate(right_parts, axis=0),
            preferred_element_type=jnp.float32,
        )

    def add_plane(rr, m, first=False, group=None):
        def step(p, carry):
            at = p if group is None else group * share + p
            if first:
                partial[at] = one_plane(rr, m, at)
            else:
                partial[at] += one_plane(rr, m, at)
            return carry

        lax.fori_loop(0, share if group is not None else depths * share, step, 0)

    def whole(rr):
        copies = []
        for n in range(1, cols):
            source = lax.rem(c + cols - n, cols)
            wait_all(chunk(0, source), right_sem.at[0, source])
            copies.extend(line(rr, 0, source))

        def take(slots):
            for n in range(cols):
                source = lax.rem(c + cols - n, cols)
                for m in slots:
                    wait_all(chunk(m, source), right_sem.at[m, source])
                    copies.extend(line(rr, m, source))

        def slots_at(far):
            return [m for m in range(1, rows) if abs((rr + m) % rows - rr) == far]

        take(slots_at(1))
        for e in range(depths):
            for m in range(0, cols, 2):
                if m or e:
                    source = lax.rem(d + depths - e, depths) * cols + lax.rem(c + cols - m, cols)
                    wait_all(left_chunk(source), left_sem.at[source])
                    copies.append(pass_left(source))
        wait_all(left_meta.at[pl.ds(0, lefts - 1)], meta_sems.at[0])
        wait_all(right_meta.at[pl.ds(0, rights - 1)], meta_sems.at[1])
        left_copy = pltpu.make_async_copy(left_meta, left_ids, local_sems.at[0])
        right_copy = pltpu.make_async_copy(right_meta, right_ids, local_sems.at[1])
        left_copy.start()
        right_copy.start()
        left_copy.wait()
        right_copy.wait()
        for e in range(depths):
            for m in range(0, cols, 2):
                source = lax.rem(d + depths - e, depths) * cols + lax.rem(other_core + cols - m, cols)
                wait_all(left_chunk(source), left_sem.at[source])
        reach = max(rr, rows - 1 - rr)
        add_plane(rr, 0, first=True)
        for m in slots_at(1):
            add_plane(rr, m)
        for far in range(2, reach + 1):
            slots = slots_at(far)
            take(slots)
            for m in slots[: None if far < reach else -1]:
                add_plane(rr, m)
        last = slots_at(reach)[-1] if reach > 1 else None
        for e in range(1, depths + 1):
            dd = lax.rem(d + e, depths)
            if last is not None:
                add_plane(rr, last, group=dd)
            if e < depths:
                copies.append(
                    remote(
                        partial.at[pl.ds(dd * share, share)],
                        arrived.at[e - 1],
                        part_send.at[e - 1],
                        part_recv.at[e - 1],
                        (r, c, dd),
                    )
                )
        for copy in copies:
            copy.wait_send()

    for rr in range(rows):
        at_row(rr, whole)

    total = partial[pl.ds(d * share, share)]
    for e in range(depths - 1):
        wait_all(arrived.at[e], part_recv.at[e])
        total = total + arrived[e]
    out_ref[...] = total

    def first_line(rr):
        for step, ahead in ((1, rr < rows - 1), (-1, rr > 0)):
            if ahead:
                wait_all(chunk(0, c), line_send.at[(step + 1) // 2, 0, c])

    for rr in range(rows):
        at_row(rr, first_line)
    for m in range(1, cols):
        wait_all(right_stage.at[m - 1], right_send.at[m - 1])
    for e in range(depths):
        for m in range(0, cols, 2):
            if m or e:
                wait_all(left_chunk(left_me), left_send.at[e, m // 2])
    for copy in passed:
        copy.wait_send()
    wait_all(left_meta.at[pl.ds(0, lefts - 1)], meta_send.at[0])
    wait_all(right_meta.at[pl.ds(0, rights - 1)], meta_send.at[1])


def body(block_values, block_cols, live_count, out_pattern):
    depths = lax.axis_size("depth")
    cols = lax.axis_size("col")
    rows = lax.axis_size("row")
    slots, size = block_values.shape[2], block_values.shape[3]
    groups = rows * depths
    blocks = groups * cols
    pair = groups // cols
    cap_left = slots // depths
    cap_right = pair * (slots // groups) + min(pair, slots % groups)
    entries = out_pattern.shape[2]
    share = entries // depths
    lefts, rights = cols * depths, rows * cols

    ids = block_cols.reshape(slots)
    order = jnp.arange(slots, dtype=jnp.int32)
    live = order < live_count.reshape(1)

    def placed(inner):
        return inner // cols % depths * rights + inner // lefts * cols + inner % cols

    def table(part, parts, cap):
        same = (part[:, None] == part[None, :]) & live[None, :]
        rank = jnp.sum((same & (order[None, :] < order[:, None])).astype(jnp.int32), axis=1)
        place = jnp.where(live, part * cap + rank, -1)
        hit = place[:, None] == jnp.arange(parts * cap, dtype=jnp.int32)[None, :]
        return jnp.sum(jnp.where(hit, order[:, None], 0), axis=0), rank

    left_index, left_rank = table(ids // cols % depths, depths, cap_left)
    right_index, right_rank = table(ids // groups, cols, cap_right)
    index = jnp.concatenate([left_index, right_index])[None]
    width = -(-blocks // 128) * 128
    mine = (placed(ids)[:, None] == jnp.arange(width, dtype=jnp.int32)[None, :]) & live[:, None]
    code = left_rank + 1 + 256 * (right_rank + 1)
    meta = jnp.sum(jnp.where(mine, code[:, None], 0), axis=0).reshape(1, 1, width)
    pattern = out_pattern.reshape(entries, 2)
    pattern = jnp.stack([pattern[:, 0] % lefts, placed(pattern[:, 1])])

    block = (size, size)
    bf16, i32 = jnp.bfloat16, jnp.int32
    vmem, smem = pltpu.VMEM, pltpu.SMEM
    dma = pltpu.SemaphoreType.DMA
    total = pl.pallas_call(
        functools.partial(kernel, (rows, cols, depths, cap_left, cap_right)),
        out_shape=jax.ShapeDtypeStruct((share,) + block, jnp.float32),
        in_specs=[pl.BlockSpec(memory_space=smem)] * 2 + [pl.BlockSpec(memory_space=vmem)] * 2,
        out_specs=pl.BlockSpec(memory_space=vmem),
        scratch_shapes=[
            vmem((depths - 1, cap_left) + block, bf16),
            vmem((cols - 1, cap_right) + block, bf16),
            vmem((lefts * cap_left,) + block, bf16),
            vmem((lefts, 1, width), i32),
            vmem((rights, 1, width), i32),
            smem((lefts, 1, width), i32),
            smem((rights, 1, width), i32),
            vmem((entries,) + block, jnp.float32),
            vmem((depths - 1, share) + block, jnp.float32),
            dma((depths, cols // 2)),
            dma((lefts,)),
            dma((lefts,)),
            dma((cols - 1,)),
            dma((rows, cols)),
            dma((2, rows, cols)),
            dma((2,)),
            dma((2,)),
            dma((2,)),
            dma((depths - 1,)),
            dma((depths - 1,)),
        ]
        + [vmem((cols * cap_right + 1,) + block, bf16)] * rows,
        compiler_params=pltpu.CompilerParams(
            collective_id=0, has_side_effects=True, vmem_limit_bytes=40 * 1024 * 1024
        ),
    )(index, pattern, meta, block_values.reshape((slots,) + block))
    return jnp.log1p(total).astype(jnp.bfloat16).reshape((1, 1, share) + block)


def solution(mesh):
    in_specs = (
        P(("row", "depth"), "col", None, None, None),
        P(("row", "depth"), "col", None),
        P(("row", "depth"), "col"),
        P("row", "col", None, None),
    )
    out_specs = P("row", "col", "depth", None, None)
    return jax.shard_map(body, mesh=mesh, in_specs=in_specs, out_specs=out_specs, check_vma=False)
```

time: 67.9 us -> 58.3 us (0.86)
  Pallas kernels: 63.4 us -> 53.9 us
    pallas_call x1, Pallas kernels: 63.4 us -> 53.9 us  [body(): pl.pallas_call(functools.partial(kernel, (rows, cols, depths, cap_left, c...]
    unnamed x7 -> x6, local copies, waits for them, and re-layouts: 2.43 us -> 2.34 us
where the time goes in v2:
time: 58.3 us; the launch traced here: 58.1 us
  Pallas kernels  53.9 us (92%)
  local copies, waits for them, and re-layouts  2.34 us (4%)
  other arithmetic  1.25 us (2%)
  between operations  0.7 us (1%)
    pallas_call x1, Pallas kernels, body(): pl.pallas_call(functools.partial(kernel, (rows, cols, depths, cap_left, c...  53.9 us
    unnamed x6, local copies, waits for them, and re-layouts  2.34 us

profile of v2, /device:TPU:0, one launch (start us, length us, event | category | flops | bytes accessed | tf_op | source)
XLA Modules:
  0.0 58.1 jit_solution(17120581142868828497)
XLA Ops:
  0.7 0.0 copy-start.1
  0.7 0.7 %copy-done.1 = s32[1,1,8,2]{2,3,1,0:T(2,128)S(1)} copy-done((s32[1,1,8,2]{2,3,1,0:T(2,128)S(1)}, s32[1,1,8,2]{2,3,1,0:T(2,128)}, u32[]{:S(2)}) %copy-start.1) | copy-done | bytes 88
  1.4 0.0 copy-start.2
  1.4 0.6 %copy-done.2 = s32[1,1,16]{2,1,0:T(1,128)S(1)} copy-done((s32[1,1,16]{2,1,0:T(1,128)S(1)}, s32[1,1,16]{2,1,0:T(1,128)}, u32[]{:S(2)}) %copy-start.2) | copy-done | bytes 88
  2.0 0.2 convert_reduce_fusion.1
  2.2 0.1 select_reduce_fusion
  2.3 0.1 select_reduce_fusion.1
  2.4 0.1 add_bitcast_fusion.index_ref
  2.5 0.0 copy-start
  2.5 1.0 %copy-done = bf16[1,1,16,128,128]{4,3,2,1,0:T(8,128)(2,1)S(1)} copy-done((bf16[1,1,16,128,128]{4,3,2,1,0:T(8,128)(2,1)S(1)}, bf16[1,1,16,128,128]{4,3,2,1,0:T(8,128)(2,1)}, u32[]{:S(2)}) %copy-start) | copy-done | bytes 524312
  3.5 53.9 %shard_map.46 = f32[4,128,128]{2,1,0:T(8,128)S(1)} custom-call(s32[1,32]{1,0:T(1,128)S(1)} %add_bitcast_fusion.index_ref, s32[2,8]{1,0:T(2,128)S(1)} %pad_add_fusion.pattern_ref, s32[1,1,128]{2,1,0:T(1,128)S(1)} %bitcast.57, bf16[16,128,128]{2,1,0:T(8,128)(2,1)S(1)} %bitcast.56), custom_call_target="tpu_custom_call" | custom-call | tf_op jit(solution)/shard_map/pallas_call | solution.py:333
  57.4 0.7 %fusion = bf16[1,1,4,128,128]{4,3,2,1,0:T(8,128)(2,1)} fusion(f32[4,128,128]{2,1,0:T(8,128)S(1)} %shard_map.46), kind=kLoop, calls=%fused_computation.1 | loop fusion | flops 65536 | bytes 393216 | tf_op jit(solution)/shard_map/reshape | solution.py:365
  (5 shorter events, 0.1 us)
Async XLA Ops:
  0.7 0.7 %copy-start.1 = (s32[1,1,8,2]{2,3,1,0:T(2,128)S(1)}, s32[1,1,8,2]{2,3,1,0:T(2,128)}, u32[]{:S(2)}) copy-start(s32[1,1,8,2]{2,3,1,0:T(2,128)} %param.7) | copy-start | bytes 196
  1.4 0.7 %copy-start.2 = (s32[1,1,16]{2,1,0:T(1,128)S(1)}, s32[1,1,16]{2,1,0:T(1,128)}, u32[]{:S(2)}) copy-start(s32[1,1,16]{2,1,0:T(1,128)} %param.5) | copy-start | bytes 196
  2.5 1.0 %copy-start = (bf16[1,1,16,128,128]{4,3,2,1,0:T(8,128)(2,1)S(1)}, bf16[1,1,16,128,128]{4,3,2,1,0:T(8,128)(2,1)}, u32[]{:S(2)}) copy-start(bf16[1,1,16,128,128]{4,3,2,1,0:T(8,128)(2,1)} %param.4) | copy-start | bytes 1572868

commit v3 on v2

v3 whole, which is shorter than its diff:
```python
import functools

import jax
import jax.numpy as jnp
from jax import lax
from jax.experimental import pallas as pl
from jax.experimental.pallas import tpu as pltpu
from jax.sharding import PartitionSpec as P

MESH = pl.DeviceIdType.MESH


def kernel(
    dims,
    index_ref,
    pattern_ref,
    meta_ref,
    values_ref,
    out_ref,
    left_stage,
    right_stage,
    left_buf,
    left_meta,
    right_meta,
    left_ids,
    right_ids,
    left_at,
    right_at,
    partial,
    arrived,
    left_send,
    left_sem,
    pass_send,
    right_send,
    right_sem,
    line_send,
    meta_send,
    meta_sems,
    local_sems,
    part_send,
    part_recv,
    *planes,
):
    rows, cols, depths, cap_left, cap_right = dims
    r, c, d = lax.axis_index("row"), lax.axis_index("col"), lax.axis_index("depth")
    left_me = d * cols + c
    right_me = r * cols + c
    share = out_ref.shape[0]
    left_total = depths * cap_left
    lefts = cols * depths
    rights = rows * cols
    zero_slot = cols * cap_right
    other_core = c + 1 - 2 * lax.rem(c, 2)

    def remote(src, dst, send, recv, to):
        copy = pltpu.make_async_remote_copy(
            src_ref=src,
            dst_ref=dst,
            send_sem=send,
            recv_sem=recv,
            device_id=to,
            device_id_type=MESH,
        )
        copy.start()
        return copy

    def wait_all(ref, sem):
        pltpu.make_async_copy(ref, ref, sem).wait()

    ranked = [sorted(range(rows), key=lambda plane: abs(plane - rr)) for rr in range(rows)]
    at_end = (r == 0) | (r == rows - 1)

    def chunk(rank, source):
        return planes[rank].at[pl.ds(source * cap_right, cap_right)]

    def left_chunk(source):
        return left_buf.at[pl.ds(source * cap_left, cap_left)]

    def column(turn, flip, sign=1):
        chips = cols // 2
        chip = lax.rem(c // 2 + chips + sign * turn, chips)
        core = lax.rem(c, 2)
        return chip * 2 + (1 - core if flip else core)

    turns = [(turn, flip) for turn in range(cols // 2) for flip in range(2)]

    barrier = pltpu.get_barrier_semaphore()
    left_peers = [(m, e) for m in range(cols) for e in range(depths) if m or e]
    right_peers = [(m, n) for n in range(rows) for m in range(cols) if m or n]

    def left_peer(m, e):
        return (r, lax.rem(c + m, cols), lax.rem(d + e, depths))

    def right_peer(m, n):
        return (lax.rem(r + n, rows), lax.rem(c + m, cols), d)

    greeted = [left_peer(m, e) for m, e in left_peers]
    greeted += [right_peer(m, n) for m, n in right_peers if n]
    for peer in greeted:
        pl.semaphore_signal(barrier, inc=1, device_id=peer, device_id_type=MESH)

    for at, (turn, flip) in enumerate(turns):
        cc = column(turn, flip)
        for q in range(cap_right):
            block = values_ref[index_ref[0, left_total + cc * cap_right + q]]
            if at == 0:
                planes[0][c * cap_right + q] = block
            else:
                right_stage[at - 1, q] = block
    left_meta[left_me] = meta_ref[0]
    right_meta[right_me] = meta_ref[0]
    for rank in range(rows):
        planes[rank][zero_slot] = jnp.zeros(planes[rank].shape[1:], planes[rank].dtype)

    pl.semaphore_wait(barrier, len(greeted))

    def hops(rr, rank):
        plane = ranked[rr][rank]
        for step, ahead in ((1, plane <= rr < rows - 1), (-1, plane >= rr > 0)):
            if ahead:
                yield step, ranked[rr + step].index(plane)

    def line(rank, source):
        def run(rr):
            for step, there in hops(rr, rank):
                remote(
                    chunk(rank, source),
                    chunk(there, source),
                    line_send.at[(step + 1) // 2, rank, source],
                    right_sem.at[there, source],
                    (r + step, c, d),
                )

        for rr in range(rows):
            if list(hops(rr, rank)):
                pl.when(r == rr)(functools.partial(run, rr))

    line(0, c)
    for at, (turn, flip) in enumerate(turns[1:]):
        remote(
            right_stage.at[at],
            chunk(0, c),
            right_send.at[at],
            right_sem.at[0, c],
            (r, column(turn, flip), d),
        )
    for m, e in left_peers:
        remote(meta_ref, left_meta.at[pl.ds(left_me, 1)], meta_send.at[0], meta_sems.at[0], left_peer(m, e))
    for m, n in right_peers:
        remote(meta_ref, right_meta.at[pl.ds(right_me, 1)], meta_send.at[1], meta_sems.at[1], right_peer(m, n))

    for e in range(depths):
        dd = lax.rem(d + e, depths)
        for q in range(cap_left):
            block = values_ref[index_ref[0, dd * cap_left + q]]
            if e == 0:
                left_buf[left_me * cap_left + q] = block
            else:
                left_stage[e - 1, q] = block

    def pass_left(source):
        return remote(
            left_chunk(source),
            left_chunk(source),
            pass_send.at[source],
            left_sem.at[source],
            (r, other_core, d),
        )

    def take(rank, source):
        wait_all(chunk(rank, source), right_sem.at[rank, source])
        line(rank, source)

    for turn, flip in turns[1:]:
        take(0, column(turn, flip, -1))

    passed = [pass_left(left_me)]
    for e in range(depths):
        for turn in range(cols // 2):
            if turn or e:
                remote(
                    left_chunk(left_me) if e == 0 else left_stage.at[e - 1],
                    left_chunk(left_me),
                    left_send.at[e, turn],
                    left_sem.at[left_me],
                    (r, column(turn, 0), lax.rem(d + e, depths)),
                )

    sources = [column(turn, flip, -1) for turn, flip in turns]

    @pl.when(jnp.logical_not(at_end))
    def _():
        for source in sources:
            take(1, source)
            take(2, source)

    wait_all(left_meta.at[pl.ds(0, lefts - 1)], meta_sems.at[0])
    wait_all(right_meta.at[pl.ds(0, rights - 1)], meta_sems.at[1])
    left_copy = pltpu.make_async_copy(left_meta, left_ids, local_sems.at[0])
    right_copy = pltpu.make_async_copy(right_meta, right_ids, local_sems.at[1])
    left_copy.start()
    right_copy.start()
    left_copy.wait()
    right_copy.wait()

    def look_up(p, carry):
        i = pattern_ref[0, p]
        j = pattern_ref[1, p]
        for inner in range(rights):
            q = lax.rem(left_ids[i, 0, d * rights + inner], 256)
            t = lax.div(right_ids[inner, 0, j], 256)
            slot = inner % cols * cap_right + t - 1
            right_at[p, inner] = jnp.where((q > 0) & (t > 0), slot, zero_slot)
            left_at[p, inner] = i * cap_left + jnp.maximum(q - 1, 0)
        return carry

    lax.fori_loop(0, depths * share, look_up, 0)

    for e in range(depths):
        for turn in range(cols // 2):
            if turn or e:
                source = lax.rem(d + depths - e, depths) * cols + column(turn, 0, -1)
                wait_all(left_chunk(source), left_sem.at[source])
                passed.append(pass_left(source))
    for e in range(depths):
        for turn in range(cols // 2):
            source = lax.rem(d + depths - e, depths) * cols + column(turn, 1, -1)
            wait_all(left_chunk(source), left_sem.at[source])

    def add_plane(rank, first, count):
        plane = jnp.int32(0)
        for rr in range(rows):
            plane = jnp.where(r == rr, ranked[rr][rank], plane)

        def step(u, carry):
            p = first + u
            left_parts, right_parts = [], []
            for source in range(cols):
                inner = plane * cols + source
                left_parts.append(left_buf[left_at[p, inner]])
                right_parts.append(planes[rank][right_at[p, inner]])
            product = jnp.dot(
                jnp.concatenate(left_parts, axis=1),
                jnp.concatenate(right_parts, axis=0),
                preferred_element_type=jnp.float32,
            )
            if rank == 0:
                partial[p] = product
            else:
                partial[p] += product
            return carry

        lax.fori_loop(0, count, step, 0, unroll=4)

    def all_chunks(rank):
        for source in sources:
            wait_all(chunk(rank, source), right_sem.at[rank, source])

    entries = depths * share
    add_plane(0, 0, entries)
    pl.when(at_end)(lambda: all_chunks(1))
    add_plane(1, 0, entries)

    @pl.when(jnp.logical_not(at_end))
    def _():
        for source in sources:
            take(3, source)

    pl.when(at_end)(lambda: all_chunks(2))
    add_plane(2, 0, entries)
    pl.when(at_end)(lambda: all_chunks(3))
    copies = []
    for e in range(1, depths + 1):
        dd = lax.rem(d + e, depths)
        add_plane(3, dd * share, share)
        if e < depths:
            copies.append(
                remote(
                    partial.at[pl.ds(dd * share, share)],
                    arrived.at[e - 1],
                    part_send.at[e - 1],
                    part_recv.at[e - 1],
                    (r, c, dd),
                )
            )
    total = partial[pl.ds(d * share, share)]
    for e, copy in enumerate(copies):
        copy.wait_recv()
        total = total + arrived[e]
    out_ref[...] = total

    for copy in copies + passed:
        copy.wait_send()

    def line_sent(rr):
        for rank in range(rows):
            for step, there in hops(rr, rank):
                for source in range(cols):
                    wait_all(chunk(rank, source), line_send.at[(step + 1) // 2, rank, source])

    for rr in range(rows):
        pl.when(r == rr)(functools.partial(line_sent, rr))
    for at in range(cols - 1):
        wait_all(right_stage.at[at], right_send.at[at])
    for e in range(depths):
        for turn in range(cols // 2):
            if turn or e:
                wait_all(left_chunk(left_me), left_send.at[e, turn])
    wait_all(left_meta.at[pl.ds(0, lefts - 1)], meta_send.at[0])
    wait_all(right_meta.at[pl.ds(0, rights - 1)], meta_send.at[1])


def body(block_values, block_cols, live_count, out_pattern):
    depths = lax.axis_size("depth")
    cols = lax.axis_size("col")
    rows = lax.axis_size("row")
    slots, size = block_values.shape[2], block_values.shape[3]
    groups = rows * depths
    blocks = groups * cols
    pair = groups // cols
    cap_left = slots // depths
    cap_right = pair * (slots // groups) + min(pair, slots % groups)
    entries = out_pattern.shape[2]
    share = entries // depths
    lefts, rights = cols * depths, rows * cols

    ids = block_cols.reshape(slots)
    order = jnp.arange(slots, dtype=jnp.int32)
    live = order < live_count.reshape(1)

    def placed(inner):
        return inner // cols % depths * rights + inner // lefts * cols + inner % cols

    def table(part, parts, cap):
        same = (part[:, None] == part[None, :]) & live[None, :]
        rank = jnp.sum((same & (order[None, :] < order[:, None])).astype(jnp.int32), axis=1)
        place = jnp.where(live, part * cap + rank, -1)
        hit = place[:, None] == jnp.arange(parts * cap, dtype=jnp.int32)[None, :]
        return jnp.sum(jnp.where(hit, order[:, None], 0), axis=0), rank

    left_index, left_rank = table(ids // cols % depths, depths, cap_left)
    right_index, right_rank = table(ids // groups, cols, cap_right)
    index = jnp.concatenate([left_index, right_index])[None]
    width = -(-blocks // 128) * 128
    mine = (placed(ids)[:, None] == jnp.arange(width, dtype=jnp.int32)[None, :]) & live[:, None]
    code = left_rank + 1 + 256 * (right_rank + 1)
    meta = jnp.sum(jnp.where(mine, code[:, None], 0), axis=0).reshape(1, 1, width)
    pattern = out_pattern.reshape(entries, 2)
    pattern = jnp.stack([pattern[:, 0] % lefts, placed(pattern[:, 1])])

    block = (size, size)
    bf16, i32 = jnp.bfloat16, jnp.int32
    vmem, smem = pltpu.VMEM, pltpu.SMEM
    dma = pltpu.SemaphoreType.DMA
    total = pl.pallas_call(
        functools.partial(kernel, (rows, cols, depths, cap_left, cap_right)),
        out_shape=jax.ShapeDtypeStruct((share,) + block, jnp.float32),
        in_specs=[pl.BlockSpec(memory_space=smem)] * 2 + [pl.BlockSpec(memory_space=vmem)] * 2,
        out_specs=pl.BlockSpec(memory_space=vmem),
        scratch_shapes=[
            vmem((depths - 1, cap_left) + block, bf16),
            vmem((cols - 1, cap_right) + block, bf16),
            vmem((lefts * cap_left,) + block, bf16),
            vmem((lefts, 1, width), i32),
            vmem((rights, 1, width), i32),
            smem((lefts, 1, width), i32),
            smem((rights, 1, width), i32),
            smem((entries, rights), i32),
            smem((entries, rights), i32),
            vmem((entries,) + block, jnp.float32),
            vmem((depths - 1, share) + block, jnp.float32),
            dma((depths, cols // 2)),
            dma((lefts,)),
            dma((lefts,)),
            dma((cols - 1,)),
            dma((rows, cols)),
            dma((2, rows, cols)),
            dma((2,)),
            dma((2,)),
            dma((2,)),
            dma((depths - 1,)),
            dma((depths - 1,)),
        ]
        + [vmem((cols * cap_right + 1,) + block, bf16)] * rows,
        compiler_params=pltpu.CompilerParams(
            collective_id=0, has_side_effects=True, vmem_limit_bytes=40 * 1024 * 1024
        ),
    )(index, pattern, meta, block_values.reshape((slots,) + block))
    return jnp.log1p(total).astype(jnp.bfloat16).reshape((1, 1, share) + block)


def solution(mesh):
    in_specs = (
        P(("row", "depth"), "col", None, None, None),
        P(("row", "depth"), "col", None),
        P(("row", "depth"), "col"),
        P("row", "col", None, None),
    )
    out_specs = P("row", "col", "depth", None, None)
    return jax.shard_map(body, mesh=mesh, in_specs=in_specs, out_specs=out_specs, check_vma=False)
```

time: 58.3 us -> 56.4 us (0.967)
  Pallas kernels: 53.9 us -> 51.9 us
    pallas_call x1, Pallas kernels: 53.9 us -> 51.9 us  [body(): pl.pallas_call(functools.partial(kernel, (rows, cols, depths, cap_left, c...]
where the time goes in v3:
time: 56.4 us; the launch traced here: 56.2 us
  Pallas kernels  51.9 us (92%)
  local copies, waits for them, and re-layouts  2.34 us (4%)
  other arithmetic  1.25 us (2%)
  between operations  0.7 us (1%)
    pallas_call x1, Pallas kernels, body(): pl.pallas_call(functools.partial(kernel, (rows, cols, depths, cap_left, c...  51.9 us
    unnamed x6, local copies, waits for them, and re-layouts  2.34 us

profile of v3, /device:TPU:0, one launch (start us, length us, event | category | flops | bytes accessed | tf_op | source)
XLA Modules:
  0.0 56.2 jit_solution(15359159257825698270)
XLA Ops:
  0.7 0.0 copy-start.1
  0.7 0.7 %copy-done.1 = s32[1,1,8,2]{2,3,1,0:T(2,128)S(1)} copy-done((s32[1,1,8,2]{2,3,1,0:T(2,128)S(1)}, s32[1,1,8,2]{2,3,1,0:T(2,128)}, u32[]{:S(2)}) %copy-start.1) | copy-done | bytes 88
  1.4 0.0 copy-start.2
  1.4 0.6 %copy-done.2 = s32[1,1,16]{2,1,0:T(1,128)S(1)} copy-done((s32[1,1,16]{2,1,0:T(1,128)S(1)}, s32[1,1,16]{2,1,0:T(1,128)}, u32[]{:S(2)}) %copy-start.2) | copy-done | bytes 88
  2.0 0.2 convert_reduce_fusion.1
  2.2 0.1 select_reduce_fusion
  2.3 0.1 select_reduce_fusion.1
  2.4 0.1 add_bitcast_fusion.index_ref
  2.5 0.0 copy-start
  2.5 1.0 %copy-done = bf16[1,1,16,128,128]{4,3,2,1,0:T(8,128)(2,1)S(1)} copy-done((bf16[1,1,16,128,128]{4,3,2,1,0:T(8,128)(2,1)S(1)}, bf16[1,1,16,128,128]{4,3,2,1,0:T(8,128)(2,1)}, u32[]{:S(2)}) %copy-start) | copy-done | bytes 524312
  3.5 51.9 %shard_map.46 = f32[4,128,128]{2,1,0:T(8,128)S(1)} custom-call(s32[1,32]{1,0:T(1,128)S(1)} %add_bitcast_fusion.index_ref, s32[2,8]{1,0:T(2,128)S(1)} %pad_add_fusion.pattern_ref, s32[1,1,128]{2,1,0:T(1,128)S(1)} %bitcast.57, bf16[16,128,128]{2,1,0:T(8,128)(2,1)S(1)} %bitcast.56), custom_call_target="tpu_custom_call" | custom-call | tf_op jit(solution)/shard_map/pallas_call | solution.py:355
  55.4 0.7 %fusion = bf16[1,1,4,128,128]{4,3,2,1,0:T(8,128)(2,1)} fusion(f32[4,128,128]{2,1,0:T(8,128)S(1)} %shard_map.46), kind=kLoop, calls=%fused_computation.1 | loop fusion | flops 65536 | bytes 393216 | tf_op jit(solution)/shard_map/reshape | solution.py:389
  (5 shorter events, 0.1 us)
Async XLA Ops:
  0.7 0.7 %copy-start.1 = (s32[1,1,8,2]{2,3,1,0:T(2,128)S(1)}, s32[1,1,8,2]{2,3,1,0:T(2,128)}, u32[]{:S(2)}) copy-start(s32[1,1,8,2]{2,3,1,0:T(2,128)} %param.7) | copy-start | bytes 196
  1.4 0.7 %copy-start.2 = (s32[1,1,16]{2,1,0:T(1,128)S(1)}, s32[1,1,16]{2,1,0:T(1,128)}, u32[]{:S(2)}) copy-start(s32[1,1,16]{2,1,0:T(1,128)} %param.5) | copy-start | bytes 196
  2.5 1.0 %copy-start = (bf16[1,1,16,128,128]{4,3,2,1,0:T(8,128)(2,1)S(1)}, bf16[1,1,16,128,128]{4,3,2,1,0:T(8,128)(2,1)}, u32[]{:S(2)}) copy-start(bf16[1,1,16,128,128]{4,3,2,1,0:T(8,128)(2,1)} %param.4) | copy-start | bytes 1572868

commit v4 on v3

--- a/solution.py
+++ b/solution.py
@@ -8,6 +8,20 @@
 from jax.sharding import PartitionSpec as P
 
 MESH = pl.DeviceIdType.MESH
+LATE = jnp.int16
+CODES = 65534.0
+TOP = 0.25
+
+
+def encode(value, bound):
+    root = jnp.sqrt(value * (1.0 / bound))
+    code = jnp.round(jnp.minimum(root, 1.0) * CODES - CODES / 2)
+    return code.astype(jnp.int32).astype(LATE)
+
+
+def decode(code, bound):
+    root = (code.astype(jnp.int32).astype(jnp.float32) + CODES / 2) * (1.0 / CODES)
+    return root * root * bound
 
 
 def kernel(
@@ -15,8 +29,9 @@
     index_ref,
     pattern_ref,
     meta_ref,
+    values_hbm,
+    out_ref,
     values_ref,
-    out_ref,
     left_stage,
     right_stage,
     left_buf,
@@ -27,7 +42,10 @@
     left_at,
     right_at,
     partial,
+    late,
+    late_mine,
     arrived,
+    late_arrived,
     left_send,
     left_sem,
     pass_send,
@@ -39,6 +57,8 @@
     local_sems,
     part_send,
     part_recv,
+    late_send,
+    late_recv,
     *planes,
 ):
     rows, cols, depths, cap_left, cap_right = dims
@@ -70,8 +90,14 @@
     ranked = [sorted(range(rows), key=lambda plane: abs(plane - rr)) for rr in range(rows)]
     at_end = (r == 0) | (r == rows - 1)
 
-    def chunk(rank, source):
-        return planes[rank].at[pl.ds(source * cap_right, cap_right)]
+    turns = [(turn, flip) for turn in range(cols // 2) for flip in range(2)]
+    half = cols // 2
+    bound = half * out_ref.shape[1] * TOP
+
+    def chunk(rank, at):
+        if rank == rows - 1 and at >= half:
+            rank = rows
+        return planes[rank].at[pl.ds(at * cap_right, cap_right)]
 
     def left_chunk(source):
         return left_buf.at[pl.ds(source * cap_left, cap_left)]
@@ -82,8 +108,8 @@
         core = lax.rem(c, 2)
         return chip * 2 + (1 - core if flip else core)
 
-    turns = [(turn, flip) for turn in range(cols // 2) for flip in range(2)]
-
+    values_copy = pltpu.make_async_copy(values_hbm, values_ref, local_sems.at[2])
+    values_copy.start()
     barrier = pltpu.get_barrier_semaphore()
     left_peers = [(m, e) for m in range(cols) for e in range(depths) if m or e]
     right_peers = [(m, n) for n in range(rows) for m in range(cols) if m or n]
@@ -99,18 +125,19 @@
     for peer in greeted:
         pl.semaphore_signal(barrier, inc=1, device_id=peer, device_id_type=MESH)
 
+    values_copy.wait()
     for at, (turn, flip) in enumerate(turns):
         cc = column(turn, flip)
         for q in range(cap_right):
             block = values_ref[index_ref[0, left_total + cc * cap_right + q]]
             if at == 0:
-                planes[0][c * cap_right + q] = block
+                planes[0][q] = block
             else:
                 right_stage[at - 1, q] = block
     left_meta[left_me] = meta_ref[0]
     right_meta[right_me] = meta_ref[0]
-    for rank in range(rows):
-        planes[rank][zero_slot] = jnp.zeros(planes[rank].shape[1:], planes[rank].dtype)
+    for plane in planes:
+        plane[zero_slot] = jnp.zeros(plane.shape[1:], plane.dtype)
 
     pl.semaphore_wait(barrier, len(greeted))
 
@@ -120,14 +147,14 @@
             if ahead:
                 yield step, ranked[rr + step].index(plane)
 
-    def line(rank, source):
+    def line(rank, at):
         def run(rr):
             for step, there in hops(rr, rank):
                 remote(
-                    chunk(rank, source),
-                    chunk(there, source),
-                    line_send.at[(step + 1) // 2, rank, source],
-                    right_sem.at[there, source],
+                    chunk(rank, at),
+                    chunk(there, at),
+                    line_send.at[(step + 1) // 2, rank, at],
+                    right_sem.at[there, at],
                     (r + step, c, d),
                 )
 
@@ -135,13 +162,13 @@
             if list(hops(rr, rank)):
                 pl.when(r == rr)(functools.partial(run, rr))
 
-    line(0, c)
+    line(0, 0)
     for at, (turn, flip) in enumerate(turns[1:]):
         remote(
             right_stage.at[at],
-            chunk(0, c),
+            chunk(0, at + 1),
             right_send.at[at],
-            right_sem.at[0, c],
+            right_sem.at[0, at + 1],
             (r, column(turn, flip), d),
         )
     for m, e in left_peers:
@@ -167,12 +194,12 @@
             (r, other_core, d),
         )
 
-    def take(rank, source):
-        wait_all(chunk(rank, source), right_sem.at[rank, source])
-        line(rank, source)
-
-    for turn, flip in turns[1:]:
-        take(0, column(turn, flip, -1))
+    def take(rank, at):
+        wait_all(chunk(rank, at), right_sem.at[rank, at])
+        line(rank, at)
+
+    for at in range(1, cols):
+        take(0, at)
 
     passed = [pass_left(left_me)]
     for e in range(depths):
@@ -190,9 +217,9 @@
 
     @pl.when(jnp.logical_not(at_end))
     def _():
-        for source in sources:
-            take(1, source)
-            take(2, source)
+        for at in range(cols):
+            take(1, at)
+            take(2, at)
 
     wait_all(left_meta.at[pl.ds(0, lefts - 1)], meta_sems.at[0])
     wait_all(right_meta.at[pl.ds(0, rights - 1)], meta_sems.at[1])
@@ -203,13 +230,18 @@
     left_copy.wait()
     right_copy.wait()
 
+    slots = []
+    for source in range(cols):
+        turn = lax.rem(c // 2 + half - source // 2, half)
+        slots.append(turn * 2 + jnp.where(lax.rem(c, 2) == source % 2, 0, 1))
+
     def look_up(p, carry):
         i = pattern_ref[0, p]
         j = pattern_ref[1, p]
         for inner in range(rights):
             q = lax.rem(left_ids[i, 0, d * rights + inner], 256)
             t = lax.div(right_ids[inner, 0, j], 256)
-            slot = inner % cols * cap_right + t - 1
+            slot = slots[inner % cols] * cap_right + t - 1
             right_at[p, inner] = jnp.where((q > 0) & (t > 0), slot, zero_slot)
             left_at[p, inner] = i * cap_left + jnp.maximum(q - 1, 0)
         return carry
@@ -227,24 +259,29 @@
             source = lax.rem(d + depths - e, depths) * cols + column(turn, 1, -1)
             wait_all(left_chunk(source), left_sem.at[source])
 
-    def add_plane(rank, first, count):
+    def add_plane(rank, first, count, ats=range(cols), last=False, mine=False):
         plane = jnp.int32(0)
         for rr in range(rows):
             plane = jnp.where(r == rr, ranked[rr][rank], plane)
+        held = planes[rows if last else rank]
 
         def step(u, carry):
             p = first + u
             left_parts, right_parts = [], []
-            for source in range(cols):
-                inner = plane * cols + source
+            for at in ats:
+                inner = plane * cols + sources[at]
                 left_parts.append(left_buf[left_at[p, inner]])
-                right_parts.append(planes[rank][right_at[p, inner]])
+                right_parts.append(held[right_at[p, inner]])
             product = jnp.dot(
                 jnp.concatenate(left_parts, axis=1),
                 jnp.concatenate(right_parts, axis=0),
                 preferred_element_type=jnp.float32,
             )
-            if rank == 0:
+            if mine:
+                late_mine[u] = product
+            elif last:
+                late[p] = encode(product, bound)
+            elif rank == 0:
                 partial[p] = product
             else:
                 partial[p] += product
@@ -252,9 +289,9 @@
 
         lax.fori_loop(0, count, step, 0, unroll=4)
 
-    def all_chunks(rank):
-        for source in sources:
-            wait_all(chunk(rank, source), right_sem.at[rank, source])
+    def all_chunks(rank, ats=range(cols)):
+        for at in ats:
+            wait_all(chunk(rank, at), right_sem.at[rank, at])
 
     entries = depths * share
     add_plane(0, 0, entries)
@@ -263,16 +300,17 @@
 
     @pl.when(jnp.logical_not(at_end))
     def _():
-        for source in sources:
-            take(3, source)
+        for at in range(cols):
+            take(rows - 1, at)
 
     pl.when(at_end)(lambda: all_chunks(2))
     add_plane(2, 0, entries)
-    pl.when(at_end)(lambda: all_chunks(3))
-    copies = []
+    early, final = range(half), range(half, cols)
+    pl.when(at_end)(lambda: all_chunks(rows - 1, early))
+    copies, late_copies = [], []
     for e in range(1, depths + 1):
         dd = lax.rem(d + e, depths)
-        add_plane(3, dd * share, share)
+        add_plane(rows - 1, dd * share, share, early)
         if e < depths:
             copies.append(
                 remote(
@@ -283,20 +321,37 @@
                     (r, c, dd),
                 )
             )
-    total = partial[pl.ds(d * share, share)]
+    pl.when(at_end)(lambda: all_chunks(rows - 1, final))
+    for e in range(1, depths + 1):
+        dd = lax.rem(d + e, depths)
+        add_plane(rows - 1, dd * share, share, final, last=True, mine=e == depths)
+        if e < depths:
+            late_copies.append(
+                remote(
+                    late.at[pl.ds(dd * share, share)],
+                    late_arrived.at[e - 1],
+                    late_send.at[e - 1],
+                    late_recv.at[e - 1],
+                    (r, c, dd),
+                )
+            )
+    total = partial[pl.ds(d * share, share)] + late_mine[...]
     for e, copy in enumerate(copies):
         copy.wait_recv()
         total = total + arrived[e]
+    for e, copy in enumerate(late_copies):
+        copy.wait_recv()
+        total = total + decode(late_arrived[e], bound)
     out_ref[...] = total
 
-    for copy in copies + passed:
+    for copy in copies + late_copies + passed:
         copy.wait_send()
 
     def line_sent(rr):
         for rank in range(rows):
             for step, there in hops(rr, rank):
-                for source in range(cols):
-                    wait_all(chunk(rank, source), line_send.at[(step + 1) // 2, rank, source])
+                for at in range(cols):
+                    wait_all(chunk(rank, at), line_send.at[(step + 1) // 2, rank, at])
 
     for rr in range(rows):
         pl.when(r == rr)(functools.partial(line_sent, rr))
@@ -355,9 +410,15 @@
     total = pl.pallas_call(
         functools.partial(kernel, (rows, cols, depths, cap_left, cap_right)),
         out_shape=jax.ShapeDtypeStruct((share,) + block, jnp.float32),
-        in_specs=[pl.BlockSpec(memory_space=smem)] * 2 + [pl.BlockSpec(memory_space=vmem)] * 2,
+        in_specs=[
+            pl.BlockSpec(memory_space=smem),
+            pl.BlockSpec(memory_space=smem),
+            pl.BlockSpec(memory_space=vmem),
+            pl.BlockSpec(memory_space=pl.ANY),
+        ],
         out_specs=pl.BlockSpec(memory_space=vmem),
         scratch_shapes=[
+            vmem((slots,) + block, bf16),
             vmem((depths - 1, cap_left) + block, bf16),
             vmem((cols - 1, cap_right) + block, bf16),
             vmem((lefts * cap_left,) + block, bf16),
@@ -368,7 +429,10 @@
             smem((entries, rights), i32),
             smem((entries, rights), i32),
             vmem((entries,) + block, jnp.float32),
+            vmem((entries,) + block, LATE),
+            vmem((share,) + block, jnp.float32),
             vmem((depths - 1, share) + block, jnp.float32),
+            vmem((depths - 1, share) + block, LATE),
             dma((depths, cols // 2)),
             dma((lefts,)),
             dma((lefts,)),
@@ -377,13 +441,15 @@
             dma((2, rows, cols)),
             dma((2,)),
             dma((2,)),
-            dma((2,)),
+            dma((3,)),
+            dma((depths - 1,)),
+            dma((depths - 1,)),
             dma((depths - 1,)),
             dma((depths - 1,)),
         ]
-        + [vmem((cols * cap_right + 1,) + block, bf16)] * rows,
+        + [vmem((cols * cap_right + 1,) + block, bf16)] * (rows + 1),
         compiler_params=pltpu.CompilerParams(
-            collective_id=0, has_side_effects=True, vmem_limit_bytes=40 * 1024 * 1024
+            collective_id=0, has_side_effects=True, vmem_limit_bytes=56 * 1024 * 1024
         ),
     )(index, pattern, meta, block_values.reshape((slots,) + block))
     return jnp.log1p(total).astype(jnp.bfloat16).reshape((1, 1, share) + block)

time: 56.4 us -> 55.5 us (0.984)
  other arithmetic: 1.25 us -> 3.86 us
  Pallas kernels: 51.9 us -> 50 us
  local copies, waits for them, and re-layouts: 2.34 us -> 0.74 us
    pallas_call x1, Pallas kernels: 51.9 us -> 50 us  [body(): pl.pallas_call(functools.partial(kernel, (rows, cols, depths, cap_left, c...]
    unnamed x6 -> x4, local copies, waits for them, and re-layouts: 2.34 us -> 0.74 us
    reshape x1, other arithmetic: 0.75 us -> 1.7 us  [body(): return jnp.log1p(total).astype(jnp.bfloat16).reshape((1, 1, share) + block)]
    broadcast_in_dim x1, other arithmetic: 0.08 us -> 0.65 us  [body(): index = jnp.concatenate([left_index, right_index])[None]]
where the time goes in v4:
time: 55.5 us; the launch traced here: 55.3 us
  Pallas kernels  50 us (90%)
  other arithmetic  3.86 us (7%)
  local copies, waits for them, and re-layouts  0.74 us (1%)
  between operations  0.69 us (1%)
    pallas_call x1, Pallas kernels, body(): pl.pallas_call(functools.partial(kernel, (rows, cols, depths, cap_left, c...  50 us
    reshape x1, other arithmetic, body(): return jnp.log1p(total).astype(jnp.bfloat16).reshape((1, 1, share) + block)  1.7 us

profile of v4, /device:TPU:0, one launch (start us, length us, event | category | flops | bytes accessed | tf_op | source)
XLA Modules:
  0.0 55.3 jit_solution(9035661859893262770)
XLA Ops:
  0.7 0.0 copy-start
  0.7 0.7 %copy-done = s32[1,1,8,2]{2,3,1,0:T(2,128)S(1)} copy-done((s32[1,1,8,2]{2,3,1,0:T(2,128)S(1)}, s32[1,1,8,2]{2,3,1,0:T(2,128)}, u32[]{:S(2)}) %copy-start) | copy-done | bytes 88
  1.4 0.0 copy-start.1
  1.4 0.6 %pad_add_fusion.pattern_ref = s32[2,8]{1,0:T(2,128)} fusion(s32[1,8]{1,0:T(1,128)S(1)} %get-tuple-element.11, s32[1,8]{1,0:T(1,128)S(1)} %get-tuple-element.10), kind=kLoop, calls=%fused_computation.29 | loop fusion | flops 16 | bytes 128 | tf_op jit(solution)/shard_map/stack | solution.py:404
  1.9 0.1 copy-done.1
  2.0 0.2 convert_reduce_fusion.1
  2.2 0.6 %select_reduce_fusion = s32[128]{0:T(128)} fusion(s32[16]{0:T(128)S(1)} %get-tuple-element.12, s32[16]{0:T(128)S(1)} %get-tuple-element.7, pred[16]{0:T(512)(128)(4,1)S(1)} %iota_compare_fusion.4), kind=kLoop, calls=%fused_computation.2 | loop fusion | flops 8064 | bytes 656 | tf_op jit(solution)/shard_map/reduce_sum | solution.py:402
  2.9 0.1 select_reduce_fusion.1
  2.9 0.6 %add_bitcast_fusion.index_ref = s32[1,32]{1,0:T(1,128)} fusion(s32[16]{0:T(128)S(1)} %get-tuple-element.15, s32[16]{0:T(128)S(1)} %get-tuple-element.16), kind=kLoop, calls=%fused_computation.47 | loop fusion | flops 32 | bytes 256 | tf_op jit(solution)/shard_map/broadcast_in_dim | solution.py:398
  3.6 50.0 %shard_map.46 = f32[4,128,128]{2,1,0:T(8,128)} custom-call(s32[1,32]{1,0:T(1,128)} %add_bitcast_fusion.index_ref, s32[2,8]{1,0:T(2,128)} %pad_add_fusion.pattern_ref, s32[1,1,128]{2,1,0:T(1,128)} %bitcast.57, bf16[16,128,128]{2,1,0:T(8,128)(2,1)} %bitcast.56), custom_call_target="tpu_custom_call" | custom-call | tf_op jit(solution)/shard_map/pallas_call | solution.py:410
  53.6 1.7 %fusion = bf16[1,1,4,128,128]{4,3,2,1,0:T(8,128)(2,1)} fusion(f32[4,128,128]{2,1,0:T(8,128)} %shard_map.46), kind=kLoop, calls=%fused_computation.1 | loop fusion | flops 65536 | bytes 393216 | tf_op jit(solution)/shard_map/reshape | solution.py:455
  (4 shorter events, 0.1 us)
Async XLA Ops:
  0.7 0.7 %copy-start = (s32[1,1,8,2]{2,3,1,0:T(2,128)S(1)}, s32[1,1,8,2]{2,3,1,0:T(2,128)}, u32[]{:S(2)}) copy-start(s32[1,1,8,2]{2,3,1,0:T(2,128)} %param.7) | copy-start | bytes 196
  1.4 0.7 %copy-start.1 = (s32[1,1,16]{2,1,0:T(1,128)S(1)}, s32[1,1,16]{2,1,0:T(1,128)}, u32[]{:S(2)}) copy-start(s32[1,1,16]{2,1,0:T(1,128)} %param.5) | copy-start | bytes 196

commit v5 on v4

--- a/solution.py
+++ b/solution.py
@@ -43,7 +43,7 @@
     right_at,
     partial,
     late,
-    late_mine,
+    late_sum,
     arrived,
     late_arrived,
     left_send,
@@ -92,7 +92,7 @@
 
     turns = [(turn, flip) for turn in range(cols // 2) for flip in range(2)]
     half = cols // 2
-    bound = half * out_ref.shape[1] * TOP
+    bound = cols * out_ref.shape[1] * TOP
 
     def chunk(rank, at):
         if rank == rows - 1 and at >= half:
@@ -194,6 +194,21 @@
             (r, other_core, d),
         )
 
+    def send_left(some):
+        for e in range(depths):
+            for turn in some:
+                if turn or e:
+                    remote(
+                        left_chunk(left_me) if e == 0 else left_stage.at[e - 1],
+                        left_chunk(left_me),
+                        left_send.at[e, turn],
+                        left_sem.at[left_me],
+                        (r, column(turn, 0), lax.rem(d + e, depths)),
+                    )
+
+    send_left(range(1))
+    passed = [pass_left(left_me)]
+
     def take(rank, at):
         wait_all(chunk(rank, at), right_sem.at[rank, at])
         line(rank, at)
@@ -201,17 +216,7 @@
     for at in range(1, cols):
         take(0, at)
 
-    passed = [pass_left(left_me)]
-    for e in range(depths):
-        for turn in range(cols // 2):
-            if turn or e:
-                remote(
-                    left_chunk(left_me) if e == 0 else left_stage.at[e - 1],
-                    left_chunk(left_me),
-                    left_send.at[e, turn],
-                    left_sem.at[left_me],
-                    (r, column(turn, 0), lax.rem(d + e, depths)),
-                )
+    send_left(range(1, cols // 2))
 
     sources = [column(turn, flip, -1) for turn, flip in turns]
 
@@ -254,6 +259,12 @@
                 source = lax.rem(d + depths - e, depths) * cols + column(turn, 0, -1)
                 wait_all(left_chunk(source), left_sem.at[source])
                 passed.append(pass_left(source))
+
+    @pl.when(jnp.logical_not(at_end))
+    def _():
+        for at in range(cols):
+            take(rows - 1, at)
+
     for e in range(depths):
         for turn in range(cols // 2):
             source = lax.rem(d + depths - e, depths) * cols + column(turn, 1, -1)
@@ -277,10 +288,12 @@
                 jnp.concatenate(right_parts, axis=0),
                 preferred_element_type=jnp.float32,
             )
-            if mine:
-                late_mine[u] = product
-            elif last:
-                late[p] = encode(product, bound)
+            if last:
+                late_sum[p] += product
+                if not mine:
+                    late[p] = encode(late_sum[p], bound)
+            elif rank == rows - 1:
+                late_sum[p] = product
             elif rank == 0:
                 partial[p] = product
             else:
@@ -298,29 +311,23 @@
     pl.when(at_end)(lambda: all_chunks(1))
     add_plane(1, 0, entries)
 
-    @pl.when(jnp.logical_not(at_end))
-    def _():
-        for at in range(cols):
-            take(rows - 1, at)
-
     pl.when(at_end)(lambda: all_chunks(2))
     add_plane(2, 0, entries)
     early, final = range(half), range(half, cols)
+    copies, late_copies = [], []
+    for e in range(1, depths):
+        dd = lax.rem(d + e, depths)
+        copies.append(
+            remote(
+                partial.at[pl.ds(dd * share, share)],
+                arrived.at[e - 1],
+                part_send.at[e - 1],
+                part_recv.at[e - 1],
+                (r, c, dd),
+            )
+        )
     pl.when(at_end)(lambda: all_chunks(rows - 1, early))
-    copies, late_copies = [], []
-    for e in range(1, depths + 1):
-        dd = lax.rem(d + e, depths)
-        add_plane(rows - 1, dd * share, share, early)
-        if e < depths:
-            copies.append(
-                remote(
-                    partial.at[pl.ds(dd * share, share)],
-                    arrived.at[e - 1],
-                    part_send.at[e - 1],
-                    part_recv.at[e - 1],
-                    (r, c, dd),
-                )
-            )
+    add_plane(rows - 1, 0, entries, early)
     pl.when(at_end)(lambda: all_chunks(rows - 1, final))
     for e in range(1, depths + 1):
         dd = lax.rem(d + e, depths)
@@ -335,7 +342,7 @@
                     (r, c, dd),
                 )
             )
-    total = partial[pl.ds(d * share, share)] + late_mine[...]
+    total = partial[pl.ds(d * share, share)] + late_sum[pl.ds(d * share, share)]
     for e, copy in enumerate(copies):
         copy.wait_recv()
         total = total + arrived[e]
@@ -430,7 +437,7 @@
             smem((entries, rights), i32),
             vmem((entries,) + block, jnp.float32),
             vmem((entries,) + block, LATE),
-            vmem((share,) + block, jnp.float32),
+            vmem((entries,) + block, jnp.float32),
             vmem((depths - 1, share) + block, jnp.float32),
             vmem((depths - 1, share) + block, LATE),
             dma((depths, cols // 2)),
@@ -449,7 +456,7 @@
         ]
         + [vmem((cols * cap_right + 1,) + block, bf16)] * (rows + 1),
         compiler_params=pltpu.CompilerParams(
-            collective_id=0, has_side_effects=True, vmem_limit_bytes=56 * 1024 * 1024
+            collective_id=0, has_side_effects=True, vmem_limit_bytes=40 * 1024 * 1024
         ),
     )(index, pattern, meta, block_values.reshape((slots,) + block))
     return jnp.log1p(total).astype(jnp.bfloat16).reshape((1, 1, share) + block)

time: 55.5 us -> 52.6 us (0.948)
  other arithmetic: 3.86 us -> 1.25 us
  Pallas kernels: 50 us -> 48.1 us
  local copies, waits for them, and re-layouts: 0.74 us -> 2.34 us
    pallas_call x1, Pallas kernels: 50 us -> 48.1 us  [body(): pl.pallas_call(functools.partial(kernel, (rows, cols, depths, cap_left, c...]
    unnamed x4 -> x6, local copies, waits for them, and re-layouts: 0.74 us -> 2.34 us
    reshape x1, other arithmetic: 1.7 us -> 0.75 us  [body(): return jnp.log1p(total).astype(jnp.bfloat16).reshape((1, 1, share) + block)]
    broadcast_in_dim x1, other arithmetic: 0.65 us -> 0.08 us  [body(): index = jnp.concatenate([left_index, right_index])[None]]
    another operation x1, other arithmetic: 0.57 us -> 0.01 us  [body(): pattern = jnp.stack([pattern[:, 0] % lefts, placed(pattern[:, 1])])]
where the time goes in v5:
time: 52.6 us; the launch traced here: 52.4 us
  Pallas kernels  48.1 us (91%)
  local copies, waits for them, and re-layouts  2.34 us (4%)
  other arithmetic  1.25 us (2%)
  between operations  0.7 us (1%)
    pallas_call x1, Pallas kernels, body(): pl.pallas_call(functools.partial(kernel, (rows, cols, depths, cap_left, c...  48.1 us
    unnamed x6, local copies, waits for them, and re-layouts  2.34 us

profile of v5, /device:TPU:0, one launch (start us, length us, event | category | flops | bytes accessed | tf_op | source)
XLA Modules:
  0.0 52.4 jit_solution(7749338314301713837)
XLA Ops:
  0.7 0.0 copy-start.1
  0.7 0.7 %copy-done.1 = s32[1,1,8,2]{2,3,1,0:T(2,128)S(1)} copy-done((s32[1,1,8,2]{2,3,1,0:T(2,128)S(1)}, s32[1,1,8,2]{2,3,1,0:T(2,128)}, u32[]{:S(2)}) %copy-start.1) | copy-done | bytes 88
  1.4 0.0 copy-start.2
  1.4 0.6 %copy-done.2 = s32[1,1,16]{2,1,0:T(1,128)S(1)} copy-done((s32[1,1,16]{2,1,0:T(1,128)S(1)}, s32[1,1,16]{2,1,0:T(1,128)}, u32[]{:S(2)}) %copy-start.2) | copy-done | bytes 88
  2.0 0.2 convert_reduce_fusion.1
  2.2 0.1 select_reduce_fusion
  2.3 0.1 select_reduce_fusion.1
  2.4 0.1 add_bitcast_fusion.index_ref
  2.5 0.0 copy-start
  2.5 1.0 %copy-done = bf16[1,1,16,128,128]{4,3,2,1,0:T(8,128)(2,1)S(1)} copy-done((bf16[1,1,16,128,128]{4,3,2,1,0:T(8,128)(2,1)S(1)}, bf16[1,1,16,128,128]{4,3,2,1,0:T(8,128)(2,1)}, u32[]{:S(2)}) %copy-start) | copy-done | bytes 524312
  3.5 48.1 %shard_map.46 = f32[4,128,128]{2,1,0:T(8,128)S(1)} custom-call(s32[1,32]{1,0:T(1,128)S(1)} %add_bitcast_fusion.index_ref, s32[2,8]{1,0:T(2,128)S(1)} %pad_add_fusion.pattern_ref, s32[1,1,128]{2,1,0:T(1,128)S(1)} %bitcast.57, bf16[16,128,128]{2,1,0:T(8,128)(2,1)S(1)} %bitcast.56), custom_call_target="tpu_custom_call" | custom-call | tf_op jit(solution)/shard_map/pallas_call | solution.py:417
  51.6 0.7 %fusion = bf16[1,1,4,128,128]{4,3,2,1,0:T(8,128)(2,1)} fusion(f32[4,128,128]{2,1,0:T(8,128)S(1)} %shard_map.46), kind=kLoop, calls=%fused_computation.1 | loop fusion | flops 65536 | bytes 393216 | tf_op jit(solution)/shard_map/reshape | solution.py:462
  (5 shorter events, 0.1 us)
Async XLA Ops:
  0.7 0.7 %copy-start.1 = (s32[1,1,8,2]{2,3,1,0:T(2,128)S(1)}, s32[1,1,8,2]{2,3,1,0:T(2,128)}, u32[]{:S(2)}) copy-start(s32[1,1,8,2]{2,3,1,0:T(2,128)} %param.7) | copy-start | bytes 196
  1.4 0.7 %copy-start.2 = (s32[1,1,16]{2,1,0:T(1,128)S(1)}, s32[1,1,16]{2,1,0:T(1,128)}, u32[]{:S(2)}) copy-start(s32[1,1,16]{2,1,0:T(1,128)} %param.5) | copy-start | bytes 196
  2.5 1.0 %copy-start = (bf16[1,1,16,128,128]{4,3,2,1,0:T(8,128)(2,1)S(1)}, bf16[1,1,16,128,128]{4,3,2,1,0:T(8,128)(2,1)}, u32[]{:S(2)}) copy-start(bf16[1,1,16,128,128]{4,3,2,1,0:T(8,128)(2,1)} %param.4) | copy-start | bytes 1572868

commit v6 on v5

--- a/solution.py
+++ b/solution.py
@@ -26,12 +26,15 @@
 
 def kernel(
     dims,
-    index_ref,
+    cols_ref,
+    live_ref,
     pattern_ref,
-    meta_ref,
     values_hbm,
     out_ref,
     values_ref,
+    index_row,
+    index_ref,
+    meta_ref,
     left_stage,
     right_stage,
     left_buf,
@@ -125,6 +128,36 @@
     for peer in greeted:
         pl.semaphore_signal(barrier, inc=1, device_id=peer, device_id_type=MESH)
 
+    def placed(inner):
+        part = lax.rem(lax.div(inner, cols), depths)
+        return part * rights + lax.div(inner, lefts) * cols + lax.rem(inner, cols)
+
+    slot_count = cols_ref.shape[1]
+    ids = [cols_ref[0, s] for s in range(slot_count)]
+    live_slots = live_ref[0, 0]
+    left_parts = [lax.rem(lax.div(k, cols), depths) for k in ids]
+    right_parts = [lax.div(k, rows * depths) for k in ids]
+    lane = lax.broadcasted_iota(jnp.int32, index_row.shape, 1)
+    wide = lax.broadcasted_iota(jnp.int32, meta_ref.shape[1:], 1)
+    index = jnp.zeros(index_row.shape, jnp.int32)
+    table = jnp.zeros(meta_ref.shape[1:], jnp.int32)
+    for s in range(slot_count):
+        left_rank, right_rank = jnp.int32(0), jnp.int32(0)
+        for before in range(s):
+            left_rank += jnp.where(left_parts[before] == left_parts[s], 1, 0)
+            right_rank += jnp.where(right_parts[before] == right_parts[s], 1, 0)
+        live = s < live_slots
+        left_to = jnp.where(live, left_parts[s] * cap_left + left_rank, -1)
+        right_to = jnp.where(live, left_total + right_parts[s] * cap_right + right_rank, -1)
+        index = jnp.where((lane == left_to) | (lane == right_to), s, index)
+        code = left_rank + 1 + 256 * (right_rank + 1)
+        table = jnp.where(wide == jnp.where(live, placed(ids[s]), -1), code, table)
+    index_row[...] = index
+    meta_ref[0] = table
+    index_copy = pltpu.make_async_copy(index_row, index_ref, local_sems.at[3])
+    index_copy.start()
+    index_copy.wait()
+
     values_copy.wait()
     for at, (turn, flip) in enumerate(turns):
         cc = column(turn, flip)
@@ -241,8 +274,8 @@
         slots.append(turn * 2 + jnp.where(lax.rem(c, 2) == source % 2, 0, 1))
 
     def look_up(p, carry):
-        i = pattern_ref[0, p]
-        j = pattern_ref[1, p]
+        i = lax.rem(pattern_ref[0, p], lefts)
+        j = placed(pattern_ref[1, p])
         for inner in range(rights):
             q = lax.rem(left_ids[i, 0, d * rights + inner], 256)
             t = lax.div(right_ids[inner, 0, j], 256)
@@ -349,7 +382,7 @@
     for e, copy in enumerate(late_copies):
         copy.wait_recv()
         total = total + decode(late_arrived[e], bound)
-    out_ref[...] = total
+    out_ref[...] = jnp.log1p(total).astype(out_ref.dtype)
 
     for copy in copies + late_copies + passed:
         copy.wait_send()
@@ -386,46 +419,28 @@
     share = entries // depths
     lefts, rights = cols * depths, rows * cols
 
-    ids = block_cols.reshape(slots)
-    order = jnp.arange(slots, dtype=jnp.int32)
-    live = order < live_count.reshape(1)
-
-    def placed(inner):
-        return inner // cols % depths * rights + inner // lefts * cols + inner % cols
-
-    def table(part, parts, cap):
-        same = (part[:, None] == part[None, :]) & live[None, :]
-        rank = jnp.sum((same & (order[None, :] < order[:, None])).astype(jnp.int32), axis=1)
-        place = jnp.where(live, part * cap + rank, -1)
-        hit = place[:, None] == jnp.arange(parts * cap, dtype=jnp.int32)[None, :]
-        return jnp.sum(jnp.where(hit, order[:, None], 0), axis=0), rank
-
-    left_index, left_rank = table(ids // cols % depths, depths, cap_left)
-    right_index, right_rank = table(ids // groups, cols, cap_right)
-    index = jnp.concatenate([left_index, right_index])[None]
     width = -(-blocks // 128) * 128
-    mine = (placed(ids)[:, None] == jnp.arange(width, dtype=jnp.int32)[None, :]) & live[:, None]
-    code = left_rank + 1 + 256 * (right_rank + 1)
-    meta = jnp.sum(jnp.where(mine, code[:, None], 0), axis=0).reshape(1, 1, width)
-    pattern = out_pattern.reshape(entries, 2)
-    pattern = jnp.stack([pattern[:, 0] % lefts, placed(pattern[:, 1])])
+    pattern = jnp.swapaxes(out_pattern, 2, 3).reshape(2, entries)
 
     block = (size, size)
     bf16, i32 = jnp.bfloat16, jnp.int32
     vmem, smem = pltpu.VMEM, pltpu.SMEM
     dma = pltpu.SemaphoreType.DMA
-    total = pl.pallas_call(
+    result = pl.pallas_call(
         functools.partial(kernel, (rows, cols, depths, cap_left, cap_right)),
-        out_shape=jax.ShapeDtypeStruct((share,) + block, jnp.float32),
+        out_shape=jax.ShapeDtypeStruct((share,) + block, bf16),
         in_specs=[
             pl.BlockSpec(memory_space=smem),
             pl.BlockSpec(memory_space=smem),
-            pl.BlockSpec(memory_space=vmem),
+            pl.BlockSpec(memory_space=smem),
             pl.BlockSpec(memory_space=pl.ANY),
         ],
         out_specs=pl.BlockSpec(memory_space=vmem),
         scratch_shapes=[
             vmem((slots,) + block, bf16),
+            vmem((1, 128), i32),
+            smem((1, 128), i32),
+            vmem((1, 1, width), i32),
             vmem((depths - 1, cap_left) + block, bf16),
             vmem((cols - 1, cap_right) + block, bf16),
             vmem((lefts * cap_left,) + block, bf16),
@@ -448,7 +463,7 @@
             dma((2, rows, cols)),
             dma((2,)),
             dma((2,)),
-            dma((3,)),
+            dma((4,)),
             dma((depths - 1,)),
             dma((depths - 1,)),
             dma((depths - 1,)),
@@ -456,10 +471,10 @@
         ]
         + [vmem((cols * cap_right + 1,) + block, bf16)] * (rows + 1),
         compiler_params=pltpu.CompilerParams(
-            collective_id=0, has_side_effects=True, vmem_limit_bytes=40 * 1024 * 1024
+            collective_id=0, has_side_effects=True, vmem_limit_bytes=56 * 1024 * 1024
         ),
-    )(index, pattern, meta, block_values.reshape((slots,) + block))
-    return jnp.log1p(total).astype(jnp.bfloat16).reshape((1, 1, share) + block)
+    )(block_cols.reshape(1, slots), live_count, pattern, block_values.reshape((slots,) + block))
+    return result.reshape((1, 1, share) + block)
 
 
 def solution(mesh):

time: 52.6 us -> 51.3 us (0.975)
  other arithmetic: 1.25 us -> 0 us
  Pallas kernels: 48.1 us -> 48.9 us
  local copies, waits for them, and re-layouts: 2.34 us -> 1.57 us
    pallas_call x1, Pallas kernels: 48.1 us -> 48.9 us  [body(): pl.pallas_call(functools.partial(kernel, (rows, cols, depths, cap_left, c...]
    unnamed x6 -> x1, local copies, waits for them, and re-layouts: 2.34 us -> 1.57 us
    reshape x1 -> x0, other arithmetic: 0.75 us -> none  [body(): return jnp.log1p(total).astype(jnp.bfloat16).reshape((1, 1, share) + block)]
where the time goes in v6:
time: 51.3 us; the launch traced here: 51.2 us
  Pallas kernels  48.9 us (95%)
  local copies, waits for them, and re-layouts  1.57 us (3%)
  between operations  0.66 us (1%)
    pallas_call x1, Pallas kernels, body(): pl.pallas_call(functools.partial(kernel, (rows, cols, depths, cap_left, c...  48.9 us
    unnamed x1, local copies, waits for them, and re-layouts  1.57 us

profile of v6, /device:TPU:0, one launch (start us, length us, event | category | flops | bytes accessed | tf_op | source)
XLA Modules:
  0.0 51.2 jit_solution(3888372232470533904)
XLA Ops:
  0.7 48.9 %shard_map.46 = bf16[4,128,128]{2,1,0:T(8,128)(2,1)} custom-call(s32[1,16]{1,0:T(1,128)} %bitcast.9, s32[1,1]{1,0:T(1,128)S(6)} %copy.6.live_ref, s32[2,8]{1,0:T(2,128)} %bitcast.8, bf16[16,128,128]{2,1,0:T(8,128)(2,1)} %bitcast.6), custom_call_target="tpu_custom_call" | custom-call | tf_op jit(solution)/shard_map/pallas_call | solution.py:429
  49.6 1.6 %copy.7 = bf16[1,1,4,128,128]{4,3,2,1,0:T(8,128)(2,1)} copy(bf16[1,1,4,128,128]{4,3,2,1,0:T(8,128)(2,1)} %bitcast.7) | data formatting | bytes 262144

commit v7 on v6

--- a/solution.py
+++ b/solution.py
@@ -196,7 +196,8 @@
                 pl.when(r == rr)(functools.partial(run, rr))
 
     line(0, 0)
-    for at, (turn, flip) in enumerate(turns[1:]):
+    for at in [*range(1, cols - 1), 0]:
+        turn, flip = turns[at + 1]
         remote(
             right_stage.at[at],
             chunk(0, at + 1),
@@ -204,11 +205,6 @@
             right_sem.at[0, at + 1],
             (r, column(turn, flip), d),
         )
-    for m, e in left_peers:
-        remote(meta_ref, left_meta.at[pl.ds(left_me, 1)], meta_send.at[0], meta_sems.at[0], left_peer(m, e))
-    for m, n in right_peers:
-        remote(meta_ref, right_meta.at[pl.ds(right_me, 1)], meta_send.at[1], meta_sems.at[1], right_peer(m, n))
-
     for e in range(depths):
         dd = lax.rem(d + e, depths)
         for q in range(cap_left):
@@ -250,6 +246,11 @@
         take(0, at)
 
     send_left(range(1, cols // 2))
+    for m, e in left_peers:
+        remote(meta_ref, left_meta.at[pl.ds(left_me, 1)], meta_send.at[0], meta_sems.at[0], left_peer(m, e))
+    for m, n in right_peers:
+        remote(meta_ref, right_meta.at[pl.ds(right_me, 1)], meta_send.at[1], meta_sems.at[1], right_peer(m, n))
+
 
     sources = [column(turn, flip, -1) for turn, flip in turns]
 
@@ -333,7 +334,7 @@
                 partial[p] += product
             return carry
 
-        lax.fori_loop(0, count, step, 0, unroll=4)
+        lax.fori_loop(0, count, step, 0, unroll=min(count, 4))
 
     def all_chunks(rank, ats=range(cols)):
         for at in ats:
@@ -362,25 +363,30 @@
     pl.when(at_end)(lambda: all_chunks(rows - 1, early))
     add_plane(rows - 1, 0, entries, early)
     pl.when(at_end)(lambda: all_chunks(rows - 1, final))
-    for e in range(1, depths + 1):
+    pieces = 2 if share % 2 == 0 else 1
+    piece = share // pieces
+    for e in range(1, depths):
         dd = lax.rem(d + e, depths)
-        add_plane(rows - 1, dd * share, share, final, last=True, mine=e == depths)
-        if e < depths:
+        for h in range(pieces):
+            begin = dd * share + h * piece
+            add_plane(rows - 1, begin, piece, final, last=True)
             late_copies.append(
                 remote(
-                    late.at[pl.ds(dd * share, share)],
-                    late_arrived.at[e - 1],
-                    late_send.at[e - 1],
-                    late_recv.at[e - 1],
+                    late.at[pl.ds(begin, piece)],
+                    late_arrived.at[e - 1, pl.ds(h * piece, piece)],
+                    late_send.at[e - 1, h],
+                    late_recv.at[e - 1, h],
                     (r, c, dd),
                 )
             )
+    add_plane(rows - 1, d * share, share, final, last=True, mine=True)
     total = partial[pl.ds(d * share, share)] + late_sum[pl.ds(d * share, share)]
     for e, copy in enumerate(copies):
         copy.wait_recv()
         total = total + arrived[e]
-    for e, copy in enumerate(late_copies):
+    for copy in late_copies:
         copy.wait_recv()
+    for e in range(depths - 1):
         total = total + decode(late_arrived[e], bound)
     out_ref[...] = jnp.log1p(total).astype(out_ref.dtype)
 
@@ -466,8 +472,8 @@
             dma((4,)),
             dma((depths - 1,)),
             dma((depths - 1,)),
-            dma((depths - 1,)),
-            dma((depths - 1,)),
+            dma((depths - 1, 2)),
+            dma((depths - 1, 2)),
         ]
         + [vmem((cols * cap_right + 1,) + block, bf16)] * (rows + 1),
         compiler_params=pltpu.CompilerParams(

time: 51.3 us -> 51.6 us (level)
  no operation moved by 1% of the time
where the time goes in v7:
time: 51.6 us; the launch traced here: 51.5 us
  Pallas kernels  49.2 us (95%)
  local copies, waits for them, and re-layouts  1.57 us (3%)
  between operations  0.66 us (1%)
    pallas_call x1, Pallas kernels, body(): pl.pallas_call(functools.partial(kernel, (rows, cols, depths, cap_left, c...  49.2 us
    unnamed x1, local copies, waits for them, and re-layouts  1.57 us

profile of v7, /device:TPU:0, one launch (start us, length us, event | category | flops | bytes accessed | tf_op | source)
XLA Modules:
  0.0 51.5 jit_solution(13303683432842955623)
XLA Ops:
  0.7 49.2 %shard_map.46 = bf16[4,128,128]{2,1,0:T(8,128)(2,1)} custom-call(s32[1,16]{1,0:T(1,128)} %bitcast.9, s32[1,1]{1,0:T(1,128)S(6)} %copy.6.live_ref, s32[2,8]{1,0:T(2,128)} %bitcast.8, bf16[16,128,128]{2,1,0:T(8,128)(2,1)} %bitcast.6), custom_call_target="tpu_custom_call" | custom-call | tf_op jit(solution)/shard_map/pallas_call | solution.py:435
  49.9 1.6 %copy.7 = bf16[1,1,4,128,128]{4,3,2,1,0:T(8,128)(2,1)} copy(bf16[1,1,4,128,128]{4,3,2,1,0:T(8,128)(2,1)} %bitcast.7) | data formatting | bytes 262144
